TPU v7x, 32 devices: a whole 2x2x4 slice. The times are simulated.
32 devices in a mesh: row: 8 (over z, y), col: 4 (over x, core).
Axes of the slice: x: 2, y: 2, z: 4, core: 2. Of those that a mesh axis runs over, the one named last changes fastest.
Arguments:
- amplitudes: float32 [4096, 2048], P('row', 'col'), may hold values from -6 to 6
- integrals: float32 [512, 2048], P('row', 'col'), may hold values from -0.1875 to 0.1875
- owner_order: int32 [512], replicated, may hold values from 0 to 511, each once
Outputs:
- cycle: float32 [512, 4096], P('col', 'row')
Inputs may be any that keep to these rules, and one draw needn't show every extreme that they name: owner_order holds each of the 512 result pairs exactly once.
All inputs are finite; a program needn't handle non-finite values.
Results may differ from a plain program's by a relative error of at most 0.00007.
Values sent between devices are 32-bit elements; how exact they have to be, the bound alone decides.
No kernel may reach another device: no remote copies, remote signals or barrier semaphores. Data moves between devices by JAX's collectives and lax.ppermute only.
A program may use at most 64 MiB of HBM per device.

v0:
```python
import jax
import jax.numpy as jnp
from jax import lax
from jax.sharding import PartitionSpec as P


def contract(left, right):
    return lax.dot_general(
        left,
        right,
        (((1,), (1,)), ((), ())),
        precision=lax.Precision.HIGHEST,
        preferred_element_type=jnp.float32,
    )


def on_device(amplitudes, integrals, owner_order):
    partial_sums = contract(lax.all_gather(integrals, "row", axis=0, tiled=True), amplitudes)
    arranged = jnp.take(partial_sums, owner_order, axis=0)
    return lax.psum_scatter(arranged, "col", scatter_dimension=0, tiled=True)


def solution(mesh):
    in_specs = (P("row", "col"), P("row", "col"), P())
    out_specs = P("col", "row")
    return jax.shard_map(
        on_device, mesh=mesh, in_specs=in_specs, out_specs=out_specs, check_vma=False
    )
```

profile of v0, /device:TPU:0, one launch (start us, length us, event | category | flops | bytes accessed | tf_op | source)
XLA Modules:
  0.0 88.9 jit_solution(16337141926609141572)
XLA Ops:
  6.5 0.0 copy-start
  6.5 0.0 copy-start.1
  6.5 0.0 all-gather.2.cloned.1.call-start
  6.5 0.7 all-gather.2.cloned.1.call-update
  7.3 0.0 reduce-scatter.2.cloned.1.call-start
  7.3 0.0 copy-done.1
  7.4 45.0 %all-gather.2.cloned.1.call-done = f32[512,512]{1,0:T(8,128)} async-done(((f32[64,512]{1,0:T(8,128)}), f32[512,512]{1,0:T(8,128)}) %all-gather.2.cloned.1.call-update) | async-done | bytes 1048592 | tf_op jit(solution)/shard_map/all_gather | solution.py:18
  52.4 0.0 copy-done
  52.4 3.1 %fusion = f32[512,512]{1,0:T(8,128)S(1)} fusion(f32[512,512]{1,0:T(8,128)} %all-gather.2.cloned.1.call-done, f32[512,512]{1,0:T(8,128)S(1)} %copy-done), kind=kOutput, calls=%fused_computation.5 | convolution fusion | flops 1610612736 | bytes 3145728 | tf_op jit(solution)/shard_map/dot_general | solution.py:8
  55.5 1.6 %gather_fusion = f32[512,512]{1,0:T(8,128)S(1)} fusion(f32[512,512]{1,0:T(8,128)S(1)} %fusion, s32[1024]{0:T(1024)S(1)} %pad_clamp_fusion), kind=kCustom, calls=%fused_computation | custom fusion | bytes 2099200 | tf_op jit(solution)/shard_map/jit(_take)/gather | solution.py:19
  57.1 1.1 %broadcast_select_fusion = f32[512,512]{1,0:T(8,128)} fusion(f32[512,512]{1,0:T(8,128)S(1)} %gather_fusion, pred[512]{0:T(512)(128)(4,1)S(1)} %compare_and_fusion), kind=kLoop, calls=%fused_computation.1 | loop fusion | flops 262144 | bytes 2097664 | tf_op jit(solution)/shard_map/jit(_take)/select_n | solution.py:19
  58.2 0.0 reduce-scatter.2.cloned.1.call-update
  58.2 23.8 %reduce-scatter.2.cloned.1.call-done = f32[128,512]{1,0:T(8,128)} async-done(((f32[512,512]{1,0:T(8,128)}), f32[128,512]{1,0:T(8,128)}) %reduce-scatter.2.cloned.1.call-update) | async-done | bytes 262160 | tf_op jit(solution)/shard_map/reduce_scatter | solution.py:20
  (3 shorter events, 0.0 us)
Async XLA Ops:
  6.5 45.8 %copy-start = (f32[512,512]{1,0:T(8,128)S(1)}, f32[512,512]{1,0:T(8,128)}, u32[]{:S(2)}) copy-start(f32[512,512]{1,0:T(8,128)} %param.3) | copy-start | bytes 3145732
  6.5 0.8 copy-start.1
  6.5 45.8 %all-gather.2.cloned.1.call-start = ((), (), s32[]{:S(2)}) async-start(), calls=%async_computation.1 | async-start | bytes 1179648 | tf_op jit(solution)/shard_map/all_gather | solution.py:18
  7.3 74.8 %reduce-scatter.2.cloned.1.call-start = ((), (), s32[]{:S(2)}) async-start(), calls=%async_computation.2 | async-start | bytes 1310720 | tf_op jit(solution)/shard_map/reduce_scatter | solution.py:20
Sparse Core Ops, SparseCore 0:
  9.5 42.8 all-gather.1
  58.4 23.6 reduce-scatter.1
where the time goes:
time: 89 us; the launch traced here: 88.9 us
  waiting for transfers between devices  69.6 us (78%)
  between operations  13.4 us (15%)
  matrix products  3.08 us (3%)
  local copies, waits for them, and re-layouts  1.63 us (2%)
  other arithmetic  1.13 us (1%)
    all_gather x1, waiting for transfers between devices, on_device(): lax.all_gather(integrals, 'row', axis=0, tiled=True)  45 us
    reduce_scatter x1, waiting for transfers between devices, on_device(): return lax.psum_scatter(arranged, 'col', scatter_dimension=0, tiled=True)  23.8 us
    dot_general x1, matrix products, contract(): lax.dot_general(left, right, (((1,), (1,)), ((), ())), precision=lax.Prec...  3.08 us
  transfers between devices with their start and end apart: 2, of which 2 were waited for; matrix products, arithmetic and copies ran while one was open for 0% of the time, Pallas kernels for 0%

commit v1 on v0

v1 whole, which is shorter than its diff:
```python
import jax
import jax.numpy as jnp
from jax import lax
from jax.experimental import pallas as pl
from jax.experimental.pallas import tpu as pltpu
from jax.sharding import PartitionSpec as P


def halves(x):
    high = x.astype(jnp.bfloat16)
    low = (x - high.astype(jnp.float32)).astype(jnp.bfloat16)
    return high, low


def times(left, right, dims):
    return lax.dot_general(left, right, (dims, ((), ())), preferred_element_type=jnp.float32)


def split_kernel(x_ref, high_ref, low_ref):
    high, low = halves(x_ref[...])
    high_ref[...] = high
    low_ref[...] = low


def split(x):
    shape = jax.ShapeDtypeStruct(x.shape, jnp.bfloat16)
    return pl.pallas_call(
        split_kernel,
        out_shape=(shape, shape),
        cost_estimate=pl.CostEstimate(flops=0, bytes_accessed=2 * x.nbytes, transcendentals=0),
    )(x)


def product_kernel(*refs):
    place_ref, high_ref, low_ref, *blocks, far_ref, near_ref, sel_high, sel_low = refs
    rows = blocks[0].shape[0]
    for m, block in enumerate(blocks):
        high, low = halves(block[...])
        sel_high[m * rows : (m + 1) * rows, :] = high
        sel_low[m * rows : (m + 1) * rows, :] = low
    for h, out in enumerate((far_ref, near_ref)):
        n = out.shape[0]
        place = place_ref[h * n : (h + 1) * n, :]
        column = lax.broadcasted_iota(jnp.int32, (n, rows * len(blocks)), 1)
        pick = jnp.where(column == place, 1.0, 0.0).astype(jnp.bfloat16)
        left_high = times(pick, sel_high[...], ((1,), (0,))).astype(jnp.bfloat16)
        left_low = times(pick, sel_low[...], ((1,), (0,))).astype(jnp.bfloat16)
        total = times(left_high, low_ref[...], ((1,), (1,)))
        total += times(left_low, high_ref[...], ((1,), (1,)))
        total += times(left_high, high_ref[...], ((1,), (1,)))
        out[...] = total


def product(place, high, low, blocks):
    n, width = place.shape[0] // 2, high.shape[0]
    depth = high.shape[1]
    stacked = len(blocks) * blocks[0].shape[0]
    shape = jax.ShapeDtypeStruct((n, width), jnp.float32)
    return pl.pallas_call(
        product_kernel,
        out_shape=(shape, shape),
        scratch_shapes=[pltpu.VMEM((stacked, depth), jnp.bfloat16)] * 2,
        compiler_params=pltpu.CompilerParams(vmem_limit_bytes=32 * 1024 * 1024),
        cost_estimate=pl.CostEstimate(
            flops=2 * n * 2 * depth * (3 * width + 2 * stacked), bytes_accessed=4 * n * width * 2, transcendentals=0
        ),
    )(place, high, low, *blocks)


def solution(mesh):
    rows, cols = mesh.shape["row"], mesh.shape["col"]

    def along(axis, size, m, x):
        return lax.ppermute(x, axis, [(i, i ^ m) for i in range(size)])

    def on_device(amplitudes, integrals, owner_order):
        high, low = split(amplitudes)
        blocks = {0: integrals}
        for m in range(rows - 2, 0, -2):
            blocks[m] = along("row", rows, m, integrals)
        for m in range(0, rows, 2):
            blocks[m + 1] = along("row", rows, 1, blocks[m])
        order = [blocks[m] for m in range(rows)]

        height = integrals.shape[0]
        me, mine = lax.axis_index("row"), lax.axis_index("col")
        local = ((owner_order // height) ^ me) * height + owner_order % height
        share = owner_order.shape[0] // cols
        local = local.reshape(cols, share)
        place = [jnp.take(local, mine ^ m, axis=0, mode="clip").reshape(share, 1) for m in range(cols)]

        out = None
        for m in range(cols - 2, -1, -2):
            other, own = product(jnp.concatenate([place[m + 1], place[m]]), high, low, order)
            own = own + along("col", cols, 1, other)
            if m:
                own = along("col", cols, m, own)
            out = own if out is None else out + own
        return out

    in_specs = (P("row", "col"), P("row", "col"), P())
    out_specs = P("col", "row")
    return jax.shard_map(
        on_device, mesh=mesh, in_specs=in_specs, out_specs=out_specs, check_vma=False
    )
```

time: 89 us -> 39.3 us (0.44)
  waiting for transfers between devices: 69.6 us -> 17.6 us
  between operations: 13.4 us -> 0.09 us
  starting transfers between devices: 0.04 us -> 11.9 us
  Pallas kernels: 0 us -> 5.54 us
  matrix products: 3.08 us -> 0 us
  local copies, waits for them, and re-layouts: 1.63 us -> 3.05 us
    all_gather x1 -> x0, waiting for transfers between devices: 45 us -> none  [on_device(): lax.all_gather(integrals, 'row', axis=0, tiled=True)]
    reduce_scatter x1 -> x0, waiting for transfers between devices: 23.8 us -> none  [on_device(): return lax.psum_scatter(arranged, 'col', scatter_dimension=0, tiled=True)]
    ppermute x0 -> x10, waiting for transfers between devices: none -> 17.6 us  [along(): return lax.ppermute(x, axis, [(i, i ^ m) for i in range(size)])]
    ppermute x0 -> x10, starting transfers between devices: none -> 11.9 us  [along(): return lax.ppermute(x, axis, [(i, i ^ m) for i in range(size)])]
    pallas_call x0 -> x3, Pallas kernels: none -> 5.54 us  [the longest x2 3.22 us: product(): pl.pallas_call(product_kernel, out_shape=(shape, shape), scratch_shapes=[...]
    dot_general x1 -> x0, matrix products: 3.08 us -> none  [contract(): lax.dot_general(left, right, (((1,), (1,)), ((), ())), precision=lax.Prec...]
    unnamed x4 -> x12, local copies, waits for them, and re-layouts: 0.01 us -> 2.78 us
    gather x1 -> x0, local copies, waits for them, and re-layouts: 1.62 us -> none  [on_device(): arranged = jnp.take(partial_sums, owner_order, axis=0)]
  transfers between devices with their start and end apart: 2 -> 10, of which waited for: 2 -> 5; matrix products, arithmetic and copies ran while one was open for 0% -> 1% of each run, Pallas kernels for 0% -> 10%
where the time goes in v1:
time: 39.3 us; the launch traced here: 39 us
  waiting for transfers between devices  17.6 us (45%)
  starting transfers between devices  11.9 us (30%)
  Pallas kernels  5.54 us (14%)
  local copies, waits for them, and re-layouts  3.05 us (8%)
  other arithmetic  0.82 us (2%)
    ppermute x10, waiting for transfers between devices, along(): return lax.ppermute(x, axis, [(i, i ^ m) for i in range(size)])  17.6 us
    ppermute x10, starting transfers between devices, along(): return lax.ppermute(x, axis, [(i, i ^ m) for i in range(size)])  11.9 us
    pallas_call x2, Pallas kernels, product(): pl.pallas_call(product_kernel, out_shape=(shape, shape), scratch_shapes=[...  3.22 us
    unnamed x12, local copies, waits for them, and re-layouts  2.78 us
    pallas_call x1, Pallas kernels, split(): pl.pallas_call(split_kernel, out_shape=(shape, shape), cost_estimate=pl.C...  2.32 us
  transfers between devices with their start and end apart: 10, of which 5 were waited for; matrix products, arithmetic and copies ran while one was open for 1% of the time, Pallas kernels for 10%

profile of v1, /device:TPU:0, one launch (start us, length us, event | category | flops | bytes accessed | tf_op | source)
XLA Modules:
  0.0 39.0 jit_solution(10780067026798572249)
XLA Ops:
  0.0 3.0 %collective-permute-start = (f32[64,512]{1,0:T(8,128)}, f32[64,512]{1,0:T(8,128)S(1)}, u32[]{:S(2)}, u32[]{:S(2)}) collective-permute-start(f32[64,512]{1,0:T(8,128)} %refs_3_.3), channel_id=1, source_target_pairs={{0,4},{4,0},{8,12},{12,8},{16,20},{20,16},{24,28},{28,24},{1,5},{5... | collective-permute-start | bytes 393224 | tf_op jit(solution)/shard_map/ppermute | solution.py:74
  3.0 1.6 %collective-permute-start.1 = (f32[64,512]{1,0:T(8,128)}, f32[64,512]{1,0:T(8,128)S(1)}, u32[]{:S(2)}, u32[]{:S(2)}) collective-permute-start(f32[64,512]{1,0:T(8,128)} %refs_3_.3), channel_id=1, source_target_pairs={{0,8},{4,12},{8,0},{12,4},{16,24},{20,28},{24,16},{28,20},{1,9},{5... | collective-permute-start | bytes 393224 | tf_op jit(solution)/shard_map/ppermute | solution.py:74
  4.5 2.6 %collective-permute-start.3 = (f32[64,512]{1,0:T(8,128)}, f32[64,512]{1,0:T(8,128)S(1)}, u32[]{:S(2)}, u32[]{:S(2)}) collective-permute-start(f32[64,512]{1,0:T(8,128)} %refs_3_.3), channel_id=1, source_target_pairs={{0,16},{4,20},{8,24},{12,28},{16,0},{20,4},{24,8},{28,12},{1,17},{... | collective-permute-start | bytes 393224 | tf_op jit(solution)/shard_map/ppermute | solution.py:74
  7.1 0.2 collective-permute-start.5
  7.4 0.0 copy-start.5
  7.4 0.7 %copy-done.5 = s32[512]{0:T(512)S(1)} copy-done((s32[512]{0:T(512)S(1)}, s32[512]{0:T(512)}, u32[]{:S(2)}) %copy-start.5) | copy-done | bytes 2072
  8.1 1.6 %collective-permute-done.1.refs_5_ = f32[64,512]{1,0:T(8,128)S(1)} collective-permute-done((f32[64,512]{1,0:T(8,128)}, f32[64,512]{1,0:T(8,128)S(1)}, u32[]{:S(2)}, u32[]{:S(2)}) %collective-permute-start.1) | collective-permute-done | bytes 131104 | tf_op jit(solution)/shard_map/ppermute | solution.py:74
  9.6 0.3 collective-permute-start.2
  9.9 7.5 %collective-permute-done.3.refs_7_ = f32[64,512]{1,0:T(8,128)S(1)} collective-permute-done((f32[64,512]{1,0:T(8,128)}, f32[64,512]{1,0:T(8,128)S(1)}, u32[]{:S(2)}, u32[]{:S(2)}) %collective-permute-start.3) | collective-permute-done | bytes 131104 | tf_op jit(solution)/shard_map/ppermute | solution.py:74
  17.4 0.5 %collective-permute-start.4 = (f32[64,512]{1,0:T(8,128)S(1)}, f32[64,512]{1,0:T(8,128)S(1)}, u32[]{:S(2)}, u32[]{:S(2)}) collective-permute-start(f32[64,512]{1,0:T(8,128)S(1)} %collective-permute-done.3.refs_7_), channel_id=1, source_target_pairs={{0,4},{4,0},{8,12},{12,8},{16,20},{20,16},{24,28},{28,24},{1,5},{5... | collective-permute-start | bytes 393224 | tf_op jit(solution)/shard_map/ppermute | solution.py:74
  17.9 0.0 collective-permute-done.5.refs_9_
  17.9 1.5 %collective-permute-start.6 = (f32[64,512]{1,0:T(8,128)S(1)}, f32[64,512]{1,0:T(8,128)S(1)}, u32[]{:S(2)}, u32[]{:S(2)}) collective-permute-start(f32[64,512]{1,0:T(8,128)S(1)} %collective-permute-done.5.refs_9_), channel_id=1, source_target_pairs={{0,4},{4,0},{8,12},{12,8},{16,20},{20,16},{24,28},{28,24},{1,5},{5... | collective-permute-start | bytes 393224 | tf_op jit(solution)/shard_map/ppermute | solution.py:74
  19.5 0.1 copy.8.refs_0_
  19.6 0.0 copy-start.4
  19.6 2.3 %shard_map.37 = (bf16[512,512]{1,0:T(8,128)(2,1)}, bf16[512,512]{1,0:T(8,128)(2,1)}) custom-call(f32[512,512]{1,0:T(8,128)} %x_ref.1), custom_call_target="tpu_custom_call" | custom-call | bytes 2097152 | tf_op jit(solution)/shard_map/pallas_call | solution.py:27
  21.9 0.0 collective-permute-done.refs_4_
  21.9 0.0 collective-permute-done.2.refs_6_
  22.0 0.4 %collective-permute-done.4.refs_8_ = f32[64,512]{1,0:T(8,128)S(1)} collective-permute-done((f32[64,512]{1,0:T(8,128)S(1)}, f32[64,512]{1,0:T(8,128)S(1)}, u32[]{:S(2)}, u32[]{:S(2)}) %collective-permute-start.4) | collective-permute-done | bytes 131104 | tf_op jit(solution)/shard_map/ppermute | solution.py:74
  22.4 1.4 %collective-permute-done.6.refs_10_ = f32[64,512]{1,0:T(8,128)S(1)} collective-permute-done((f32[64,512]{1,0:T(8,128)S(1)}, f32[64,512]{1,0:T(8,128)S(1)}, u32[]{:S(2)}, u32[]{:S(2)}) %collective-permute-start.6) | collective-permute-done | bytes 131104 | tf_op jit(solution)/shard_map/ppermute | solution.py:74
  23.8 0.0 copy-done.4
  23.8 0.0 copy-start
  23.8 1.0 %copy-done = bf16[512,512]{1,0:T(8,128)(2,1)S(1)} copy-done((bf16[512,512]{1,0:T(8,128)(2,1)S(1)}, bf16[512,512]{1,0:T(8,128)(2,1)}, u32[]{:S(2)}) %copy-start) | copy-done | bytes 524312
  24.8 0.0 copy-start.2
  24.8 1.0 %copy-done.2 = bf16[512,512]{1,0:T(8,128)(2,1)S(1)} copy-done((bf16[512,512]{1,0:T(8,128)(2,1)S(1)}, bf16[512,512]{1,0:T(8,128)(2,1)}, u32[]{:S(2)}) %copy-start.2) | copy-done | bytes 524312
  25.9 0.0 copy-start.1
  25.9 0.0 copy-start.3
  25.9 1.6 %shard_map.38 = (f32[128,512]{1,0:T(8,128)S(1)}, f32[128,512]{1,0:T(8,128)S(1)}) custom-call(s32[256,1]{1,0:T(8,128)S(1)} %copy.8.refs_0_, bf16[512,512]{1,0:T(8,128)(2,1)S(1)} %copy-done, bf16[512,512]{1,0:T(8,128)(2,1)S(1)} %copy-done.2, f32[64,512]{1,0:T(8,128)S(1)} %copy-done.4, f32[64,512]{1,0:T(8,128)S(1)} %collective-permute-done.refs_4_, ...), custom_call_target="tpu_custom_call" | custom-call | flops 671088640 | bytes 524288 | tf_op jit(solution)/shard_map/pallas_call | solution.py:59
  27.5 0.1 collective-permute-start.7
  27.6 0.1 copy.9.refs_0_
  27.7 0.0 copy-done.1
  27.7 0.0 copy-done.3
  27.7 1.6 %shard_map.39 = (f32[128,512]{1,0:T(8,128)S(1)}, f32[128,512]{1,0:T(8,128)S(1)}) custom-call(s32[256,1]{1,0:T(8,128)S(1)} %copy.9.refs_0_, bf16[512,512]{1,0:T(8,128)(2,1)S(1)} %copy-done.1, bf16[512,512]{1,0:T(8,128)(2,1)S(1)} %copy-done.3, f32[64,512]{1,0:T(8,128)S(1)} %copy-done.4, f32[64,512]{1,0:T(8,128)S(1)} %collective-permute-done.refs_4_, ...), custom_call_target="tpu_custom_call" | custom-call | flops 671088640 | bytes 524288 | tf_op jit(solution)/shard_map/pallas_call | solution.py:59
  29.4 0.6 %collective-permute-start.9 = (f32[128,512]{1,0:T(8,128)S(1)}, f32[128,512]{1,0:T(8,128)S(1)}, u32[]{:S(2)}, u32[]{:S(2)}) collective-permute-start(f32[128,512]{1,0:T(8,128)S(1)} %get-tuple-element.16), channel_id=1, source_target_pairs={{0,1},{1,0},{2,3},{3,2},{4,5},{5,4},{6,7},{7,6},{8,9},{9,8},{10,11... | collective-permute-start | bytes 786440 | tf_op jit(solution)/shard_map/ppermute | solution.py:74
  29.9 0.0 collective-permute-done.7
  30.0 1.6 %collective-permute-start.8 = (f32[128,512]{1,0:T(8,128)S(1)}, f32[128,512]{1,0:T(8,128)S(1)}, u32[]{:S(2)}, u32[]{:S(2)}) collective-permute-start(f32[128,512]{1,0:T(8,128)S(1)} %add.21), channel_id=1, source_target_pairs={{0,2},{1,3},{2,0},{3,1},{4,6},{5,7},{6,4},{7,5},{8,10},{9,11},{10,... | collective-permute-start | bytes 786440 | tf_op jit(solution)/shard_map/ppermute | solution.py:74
  31.5 0.0 collective-permute-done.9
  31.5 6.7 %collective-permute-done.8 = f32[128,512]{1,0:T(8,128)S(1)} collective-permute-done((f32[128,512]{1,0:T(8,128)S(1)}, f32[128,512]{1,0:T(8,128)S(1)}, u32[]{:S(2)}, u32[]{:S(2)}) %collective-permute-start.8) | collective-permute-done | bytes 262176 | tf_op jit(solution)/shard_map/ppermute | solution.py:74
  38.3 0.8 %add_add_fusion = f32[128,512]{1,0:T(8,128)} fusion(f32[128,512]{1,0:T(8,128)S(1)} %collective-permute-done.8, f32[128,512]{1,0:T(8,128)S(1)} %get-tuple-element.15, f32[128,512]{1,0:T(8,128)S(1)} %collective-permute-done.9), kind=kLoop, calls=%fused_computation | loop fusion | flops 131072 | bytes 1048576 | tf_op jit(solution)/shard_map/add | solution.py:98
  (4 shorter events, 0.1 us)
Async XLA Ops:
  0.0 21.9 %collective-permute-start = (f32[64,512]{1,0:T(8,128)}, f32[64,512]{1,0:T(8,128)S(1)}, u32[]{:S(2)}, u32[]{:S(2)}) collective-permute-start(f32[64,512]{1,0:T(8,128)} %refs_3_.3), channel_id=1, source_target_pairs={{0,4},{4,0},{8,12},{12,8},{16,20},{20,16},{24,28},{28,24},{1,5},{5... | collective-permute-start | bytes 393224 | tf_op jit(solution)/shard_map/ppermute | solution.py:74
  3.0 6.6 %collective-permute-start.1 = (f32[64,512]{1,0:T(8,128)}, f32[64,512]{1,0:T(8,128)S(1)}, u32[]{:S(2)}, u32[]{:S(2)}) collective-permute-start(f32[64,512]{1,0:T(8,128)} %refs_3_.3), channel_id=1, source_target_pairs={{0,8},{4,12},{8,0},{12,4},{16,24},{20,28},{24,16},{28,20},{1,9},{5... | collective-permute-start | bytes 393224 | tf_op jit(solution)/shard_map/ppermute | solution.py:74
  4.5 12.9 %collective-permute-start.3 = (f32[64,512]{1,0:T(8,128)}, f32[64,512]{1,0:T(8,128)S(1)}, u32[]{:S(2)}, u32[]{:S(2)}) collective-permute-start(f32[64,512]{1,0:T(8,128)} %refs_3_.3), channel_id=1, source_target_pairs={{0,16},{4,20},{8,24},{12,28},{16,0},{20,4},{24,8},{28,12},{1,17},{... | collective-permute-start | bytes 393224 | tf_op jit(solution)/shard_map/ppermute | solution.py:74
  7.1 10.8 %collective-permute-start.5 = (f32[64,512]{1,0:T(8,128)}, f32[64,512]{1,0:T(8,128)S(1)}, u32[]{:S(2)}, u32[]{:S(2)}) collective-permute-start(f32[64,512]{1,0:T(8,128)} %refs_3_.3), channel_id=1, source_target_pairs={{0,24},{4,28},{8,16},{12,20},{16,8},{20,12},{24,0},{28,4},{1,25},{... | collective-permute-start | bytes 393224 | tf_op jit(solution)/shard_map/ppermute | solution.py:74
  7.4 0.7 %copy-start.5 = (s32[512]{0:T(512)S(1)}, s32[512]{0:T(512)}, u32[]{:S(2)}) copy-start(s32[512]{0:T(512)} %param.5) | copy-start | bytes 6148
  9.6 12.3 %collective-permute-start.2 = (f32[64,512]{1,0:T(8,128)S(1)}, f32[64,512]{1,0:T(8,128)S(1)}, u32[]{:S(2)}, u32[]{:S(2)}) collective-permute-start(f32[64,512]{1,0:T(8,128)S(1)} %collective-permute-done.1.refs_5_), channel_id=1, source_target_pairs={{0,4},{4,0},{8,12},{12,8},{16,20},{20,16},{24,28},{28,24},{1,5},{5... | collective-permute-start | bytes 393224 | tf_op jit(solution)/shard_map/ppermute | solution.py:74
  17.4 5.0 %collective-permute-start.4 = (f32[64,512]{1,0:T(8,128)S(1)}, f32[64,512]{1,0:T(8,128)S(1)}, u32[]{:S(2)}, u32[]{:S(2)}) collective-permute-start(f32[64,512]{1,0:T(8,128)S(1)} %collective-permute-done.3.refs_7_), channel_id=1, source_target_pairs={{0,4},{4,0},{8,12},{12,8},{16,20},{20,16},{24,28},{28,24},{1,5},{5... | collective-permute-start | bytes 393224 | tf_op jit(solution)/shard_map/ppermute | solution.py:74
  17.9 5.9 %collective-permute-start.6 = (f32[64,512]{1,0:T(8,128)S(1)}, f32[64,512]{1,0:T(8,128)S(1)}, u32[]{:S(2)}, u32[]{:S(2)}) collective-permute-start(f32[64,512]{1,0:T(8,128)S(1)} %collective-permute-done.5.refs_9_), channel_id=1, source_target_pairs={{0,4},{4,0},{8,12},{12,8},{16,20},{20,16},{24,28},{28,24},{1,5},{5... | collective-permute-start | bytes 393224 | tf_op jit(solution)/shard_map/ppermute | solution.py:74
  19.6 4.2 %copy-start.4 = (f32[64,512]{1,0:T(8,128)S(1)}, f32[64,512]{1,0:T(8,128)}, u32[]{:S(2)}) copy-start(f32[64,512]{1,0:T(8,128)} %refs_3_.3) | copy-start | bytes 393220
  23.8 1.0 %copy-start = (bf16[512,512]{1,0:T(8,128)(2,1)S(1)}, bf16[512,512]{1,0:T(8,128)(2,1)}, u32[]{:S(2)}) copy-start(bf16[512,512]{1,0:T(8,128)(2,1)} %get-tuple-element.11.refs_1_) | copy-start | bytes 1572868
  24.8 1.0 %copy-start.2 = (bf16[512,512]{1,0:T(8,128)(2,1)S(1)}, bf16[512,512]{1,0:T(8,128)(2,1)}, u32[]{:S(2)}) copy-start(bf16[512,512]{1,0:T(8,128)(2,1)} %get-tuple-element.12.refs_2_) | copy-start | bytes 1572868
  25.9 1.8 %copy-start.1 = (bf16[512,512]{1,0:T(8,128)(2,1)S(1)}, bf16[512,512]{1,0:T(8,128)(2,1)}, u32[]{:S(2)}) copy-start(bf16[512,512]{1,0:T(8,128)(2,1)} %get-tuple-element.11.refs_1_) | copy-start | bytes 1572868
  25.9 1.8 %copy-start.3 = (bf16[512,512]{1,0:T(8,128)(2,1)S(1)}, bf16[512,512]{1,0:T(8,128)(2,1)}, u32[]{:S(2)}) copy-start(bf16[512,512]{1,0:T(8,128)(2,1)} %get-tuple-element.12.refs_2_) | copy-start | bytes 1572868
  27.5 2.4 %collective-permute-start.7 = (f32[128,512]{1,0:T(8,128)S(1)}, f32[128,512]{1,0:T(8,128)S(1)}, u32[]{:S(2)}, u32[]{:S(2)}) collective-permute-start(f32[128,512]{1,0:T(8,128)S(1)} %get-tuple-element.14), channel_id=1, source_target_pairs={{0,1},{1,0},{2,3},{3,2},{4,5},{5,4},{6,7},{7,6},{8,9},{9,8},{10,11... | collective-permute-start | bytes 786440 | tf_op jit(solution)/shard_map/ppermute | solution.py:74
  29.4 2.2 %collective-permute-start.9 = (f32[128,512]{1,0:T(8,128)S(1)}, f32[128,512]{1,0:T(8,128)S(1)}, u32[]{:S(2)}, u32[]{:S(2)}) collective-permute-start(f32[128,512]{1,0:T(8,128)S(1)} %get-tuple-element.16), channel_id=1, source_target_pairs={{0,1},{1,0},{2,3},{3,2},{4,5},{5,4},{6,7},{7,6},{8,9},{9,8},{10,11... | collective-permute-start | bytes 786440 | tf_op jit(solution)/shard_map/ppermute | solution.py:74
  30.0 8.3 %collective-permute-start.8 = (f32[128,512]{1,0:T(8,128)S(1)}, f32[128,512]{1,0:T(8,128)S(1)}, u32[]{:S(2)}, u32[]{:S(2)}) collective-permute-start(f32[128,512]{1,0:T(8,128)S(1)} %add.21), channel_id=1, source_target_pairs={{0,2},{1,3},{2,0},{3,1},{4,6},{5,7},{6,4},{7,5},{8,10},{9,11},{10,... | collective-permute-start | bytes 786440 | tf_op jit(solution)/shard_map/ppermute | solution.py:74

commit v2 on v0

v2 whole, which is shorter than its diff:
```python
import functools

import jax
import jax.numpy as jnp
from jax import lax
from jax.experimental import pallas as pl
from jax.experimental.pallas import tpu as pltpu
from jax.sharding import PartitionSpec as P

MIB = 1024 * 1024


def halves(x):
    high = x.astype(jnp.bfloat16)
    low = (x - high.astype(jnp.float32)).astype(jnp.bfloat16)
    return high, low


def times(left, right):
    return lax.dot_general(left, right, (((1,), (0,)), ((), ())), preferred_element_type=jnp.float32)


def prepare_kernel(x_ref, place_ref, right_ref, pick_ref):
    high, low = halves(x_ref[...].T)
    depth = high.shape[0]
    right_ref[:depth, :] = high
    right_ref[depth : 2 * depth, :] = high
    right_ref[2 * depth :, :] = low
    column = lax.broadcasted_iota(jnp.int32, pick_ref.shape, 1)
    pick_ref[...] = jnp.where(column == place_ref[...], 1.0, 0.0).astype(jnp.bfloat16)


def prepare(amplitudes, place, stacked):
    width, depth = amplitudes.shape
    return pl.pallas_call(
        prepare_kernel,
        out_shape=(
            jax.ShapeDtypeStruct((3 * depth, width), jnp.bfloat16),
            jax.ShapeDtypeStruct((place.shape[0], stacked), jnp.bfloat16),
        ),
        compiler_params=pltpu.CompilerParams(vmem_limit_bytes=8 * MIB),
        cost_estimate=pl.CostEstimate(flops=0, bytes_accessed=4 * MIB, transcendentals=0),
    )(amplitudes, place)


def product_kernel(spots, pick_ref, right_ref, *refs):
    *pieces, other_ref, own_ref, parts, left = refs
    depth = pieces[0].shape[1]
    for piece, moves in zip(pieces, spots):
        for source, target, n in moves:
            high, low = halves(piece[source : source + n, :])
            parts[target : target + n, :depth] = high
            parts[target : target + n, depth:] = low
    chosen = times(pick_ref[...], parts[...]).astype(jnp.bfloat16)
    left[:, : 2 * depth] = chosen
    left[:, 2 * depth :] = chosen[:, :depth]
    total = times(left[...], right_ref[...])
    n = other_ref.shape[0]
    other_ref[...] = total[:n]
    own_ref[...] = total[n:]


def product(pick, right, placed):
    n, stacked = pick.shape
    pieces = [piece for piece, _ in placed]
    spots = [moves for _, moves in placed]
    width, depth = right.shape[1], pieces[0].shape[1]
    shape = jax.ShapeDtypeStruct((n // 2, width), jnp.float32)
    return pl.pallas_call(
        functools.partial(product_kernel, spots),
        out_shape=(shape, shape),
        scratch_shapes=[
            pltpu.VMEM((stacked, 2 * depth), jnp.bfloat16),
            pltpu.VMEM((n, 3 * depth), jnp.bfloat16),
        ],
        compiler_params=pltpu.CompilerParams(vmem_limit_bytes=8 * MIB),
        cost_estimate=pl.CostEstimate(
            flops=2 * n * depth * (3 * width + 2 * stacked), bytes_accessed=4 * MIB, transcendentals=0
        ),
    )(pick, right, *pieces)


def solution(mesh):
    rows, cols = mesh.shape["row"], mesh.shape["col"]

    def along(axis, size, m, x):
        return lax.ppermute(x, axis, [(i, i ^ m) for i in range(size)])

    def on_device(amplitudes, integrals, owner_order):
        height = integrals.shape[0]
        stacked = rows * height
        me, mine = lax.axis_index("row"), lax.axis_index("col")
        local = ((owner_order // height) ^ me) * height + owner_order % height
        share = stacked // cols
        local = local.reshape(cols, share)
        place = jnp.concatenate([jnp.take(local, mine ^ m, axis=0, mode="clip") for m in range(cols - 1, -1, -1)])
        right, pick = prepare(amplitudes, place.reshape(stacked, 1), stacked)

        far = rows // 2
        cut = height // 32 * 16 or height
        near, wide = range(2, far, 2), range(far + 2, rows, 2)
        got = {0: integrals}
        for m in near:
            got[m] = along("row", rows, m, integrals)
        top = along("row", rows, far, integrals[:cut])
        for m in near:
            got[m + 1] = along("row", rows, 1, got[m])
        got[1] = along("row", rows, 1, integrals)
        for m in wide:
            got[m] = along("row", rows, m, integrals)
        if cut < height:
            below = along("row", rows, far, jnp.concatenate([integrals[cut:], got[1][cut:]]))
        for m in wide:
            got[m + 1] = along("row", rows, 1, got[m])
        if near:
            top, got[near[-1] + 1] = lax.optimization_barrier((top, got[near[-1] + 1]))
        top_next = along("row", rows, 1, top)
        order = [0, *near, *[m + 1 for m in wide], *[m + 1 for m in near], *wide]
        placed = [(got[m], [(0, m * height, height)]) for m in order]
        placed.append((top_next, [(0, (far + 1) * height, cut)]))
        placed.append((top, [(0, far * height, cut)]))
        placed.append((got[1], [(0, height, height)]))
        if cut < height:
            rest = height - cut
            placed.append((below, [(0, far * height + cut, rest), (rest, (far + 1) * height + cut, rest)]))

        if height % 16:
            placed.sort(key=lambda item: item[1][0][1])
            placed = [(jnp.concatenate([piece for piece, _ in placed]), [(0, 0, stacked)])]
        sums = []
        for step in range(cols // 2):
            chosen = pick[2 * step * share : 2 * (step + 1) * share]
            other, own = product(chosen, right, placed)
            sums.append(own + along("col", cols, 1, other))
        out = sums.pop()
        for step, total in enumerate(sums):
            out = out + along("col", cols, cols - 2 - 2 * step, total)
        return out

    in_specs = (P("row", "col"), P("row", "col"), P())
    out_specs = P("col", "row")
    return jax.shard_map(
        on_device, mesh=mesh, in_specs=in_specs, out_specs=out_specs, check_vma=False
    )
```

time: 89 us -> 32.4 us (0.36)
  waiting for transfers between devices: 69.6 us -> 9.84 us
  starting transfers between devices: 0.04 us -> 16.3 us
  between operations: 13.4 us -> 0.12 us
  matrix products: 3.08 us -> 0 us
  Pallas kernels: 0 us -> 2.18 us
    all_gather x1 -> x0, waiting for transfers between devices: 45 us -> none  [on_device(): lax.all_gather(integrals, 'row', axis=0, tiled=True)]
    reduce_scatter x1 -> x0, waiting for transfers between devices: 23.8 us -> none  [on_device(): return lax.psum_scatter(arranged, 'col', scatter_dimension=0, tiled=True)]
    ppermute x0 -> x11, starting transfers between devices: none -> 16.3 us  [along(): return lax.ppermute(x, axis, [(i, i ^ m) for i in range(size)])]
    ppermute x0 -> x11, waiting for transfers between devices: none -> 9.84 us  [along(): return lax.ppermute(x, axis, [(i, i ^ m) for i in range(size)])]
    dot_general x1 -> x0, matrix products: 3.08 us -> none  [contract(): lax.dot_general(left, right, (((1,), (1,)), ((), ())), precision=lax.Prec...]
    pallas_call x0 -> x3, Pallas kernels: none -> 2.18 us  [the longest x2 1.73 us: product(): pl.pallas_call(functools.partial(product_kernel, spots), out_shape=(shape...]
    gather x1, local copies, waits for them, and re-layouts: 1.62 us -> 0.01 us  [on_device(): jnp.take(local, mine ^ m, axis=0, mode='clip')]
    unnamed x4, local copies, waits for them, and re-layouts: 0.01 us -> 1.23 us
  transfers between devices with their start and end apart: 2 -> 11, of which waited for: 2 -> 6; matrix products, arithmetic and copies ran while one was open for 0% -> 6% of each run, Pallas kernels for 0% -> 4%
where the time goes in v2:
time: 32.4 us; the launch traced here: 32.2 us
  starting transfers between devices  16.3 us (50%)
  waiting for transfers between devices  9.84 us (30%)
  local copies, waits for them, and re-layouts  2.31 us (7%)
  Pallas kernels  2.18 us (7%)
  other arithmetic  1.51 us (5%)
    ppermute x11, starting transfers between devices, along(): return lax.ppermute(x, axis, [(i, i ^ m) for i in range(size)])  16.3 us
    ppermute x11, waiting for transfers between devices, along(): return lax.ppermute(x, axis, [(i, i ^ m) for i in range(size)])  9.84 us
    pallas_call x2, Pallas kernels, product(): pl.pallas_call(functools.partial(product_kernel, spots), out_shape=(shape...  1.73 us
    unnamed x4, local copies, waits for them, and re-layouts  1.23 us
    slice x1, local copies, waits for them, and re-layouts, on_device(): integrals[cut:]  0.88 us
    add x1, other arithmetic, on_device(): out = out + along('col', cols, cols - 2 - 2 * step, total)  0.76 us
    reshape x1, other arithmetic, on_device(): local = local.reshape(cols, share)  0.69 us
  transfers between devices with their start and end apart: 11, of which 6 were waited for; matrix products, arithmetic and copies ran while one was open for 6% of the time, Pallas kernels for 4%

profile of v2, /device:TPU:0, one launch (start us, length us, event | category | flops | bytes accessed | tf_op | source)
XLA Modules:
  0.0 32.2 jit_solution(3419967379238443354)
XLA Ops:
  0.0 3.0 %collective-permute-start = (f32[64,512]{1,0:T(8,128)}, f32[64,512]{1,0:T(8,128)S(1)}, u32[]{:S(2)}, u32[]{:S(2)}) collective-permute-start(f32[64,512]{1,0:T(8,128)} %refs_0_.3), channel_id=1, source_target_pairs={{0,8},{4,12},{8,0},{12,4},{16,24},{20,28},{24,16},{28,20},{1,9},{5... | collective-permute-start | bytes 393224 | tf_op jit(solution)/shard_map/ppermute | solution.py:87
  3.0 2.5 %collective-permute-start.1 = (f32[64,512]{1,0:T(8,128)}, f32[64,512]{1,0:T(8,128)S(1)}, u32[]{:S(2)}, u32[]{:S(2)}) collective-permute-start(f32[64,512]{1,0:T(8,128)} %refs_0_.3), channel_id=1, source_target_pairs={{0,24},{4,28},{8,16},{12,20},{16,8},{20,12},{24,0},{28,4},{1,25},{... | collective-permute-start | bytes 393224 | tf_op jit(solution)/shard_map/ppermute | solution.py:87
  5.5 1.5 %collective-permute-start.6 = (f32[64,512]{1,0:T(8,128)}, f32[64,512]{1,0:T(8,128)S(1)}, u32[]{:S(2)}, u32[]{:S(2)}) collective-permute-start(f32[64,512]{1,0:T(8,128)} %refs_0_.3), channel_id=1, source_target_pairs={{0,4},{4,0},{8,12},{12,8},{16,20},{20,16},{24,28},{28,24},{1,5},{5... | collective-permute-start | bytes 393224 | tf_op jit(solution)/shard_map/ppermute | solution.py:87
  7.0 0.9 %fusion.11 = (f32[32,512]{1,0:T(8,128)S(1)}, f32[32,512]{1,0:T(8,128)S(1)}) fusion(f32[64,512]{1,0:T(8,128)} %refs_0_.3), kind=kLoop, calls=%fused_computation.24 | loop fusion | bytes 262144 | tf_op jit(solution)/shard_map/slice | solution.py:112
  7.9 0.0 copy-start
  7.9 0.2 collective-permute-start.3
  8.1 0.7 %fusion.3 = s32[4,128]{1,0:T(4,128)S(1)} fusion(s32[512]{0:T(512)} %param.5, s32[]{:T(128)S(6)} %axis_index.23), kind=kLoop, calls=%fused_computation.10 | loop fusion | flops 11264 | bytes 4100 | tf_op jit(solution)/shard_map/reshape | solution.py:95
  8.8 0.0 collective-permute-done.refs_1_
  8.8 0.6 %collective-permute-start.4 = (f32[64,512]{1,0:T(8,128)S(1)}, f32[64,512]{1,0:T(8,128)S(1)}, u32[]{:S(2)}, u32[]{:S(2)}) collective-permute-start(f32[64,512]{1,0:T(8,128)S(1)} %collective-permute-done.refs_1_), channel_id=1, source_target_pairs={{0,4},{4,0},{8,12},{12,8},{16,20},{20,16},{24,28},{28,24},{1,5},{5... | collective-permute-start | bytes 393224 | tf_op jit(solution)/shard_map/ppermute | solution.py:87
  9.4 0.1 copy.4.place_ref
  9.6 0.0 copy-start.1
  9.6 1.2 %copy-done.1 = f32[512,512]{1,0:T(8,128)S(1)} copy-done((f32[512,512]{1,0:T(8,128)S(1)}, f32[512,512]{1,0:T(8,128)}, u32[]{:S(2)}) %copy-start.1) | copy-done | bytes 1048600
  10.8 0.4 %shard_map.37 = (bf16[1536,512]{1,0:T(8,128)(2,1)S(1)}, bf16[512,512]{1,0:T(8,128)(2,1)S(1)}) custom-call(f32[512,512]{1,0:T(8,128)S(1)} %copy-done.1, s32[512,1]{1,0:T(8,128)S(1)} %copy.4.place_ref), custom_call_target="tpu_custom_call" | custom-call | bytes 4194304 | tf_op jit(solution)/shard_map/pallas_call | solution.py:35
  11.3 0.0 collective-permute-done.6.refs_7_
  11.3 2.9 %collective-permute-start.7 = (f32[64,512]{1,0:T(8,128)S(1)}, f32[64,512]{1,0:T(8,128)S(1)}, u32[]{:S(2)}, u32[]{:S(2)}) collective-permute-start(f32[64,512]{1,0:T(8,128)S(1)} %pad_maximum_fusion), channel_id=1, source_target_pairs={{0,16},{4,20},{8,24},{12,28},{16,0},{20,4},{24,8},{28,12},{1,17},{... | collective-permute-start | bytes 393224 | tf_op jit(solution)/shard_map/ppermute | solution.py:87
  14.2 0.0 collective-permute-done.1.refs_4_
  14.2 1.5 %collective-permute-start.2 = (f32[64,512]{1,0:T(8,128)S(1)}, f32[64,512]{1,0:T(8,128)S(1)}, u32[]{:S(2)}, u32[]{:S(2)}) collective-permute-start(f32[64,512]{1,0:T(8,128)S(1)} %collective-permute-done.1.refs_4_), channel_id=1, source_target_pairs={{0,4},{4,0},{8,12},{12,8},{16,20},{20,16},{24,28},{28,24},{1,5},{5... | collective-permute-start | bytes 393224 | tf_op jit(solution)/shard_map/ppermute | solution.py:87
  15.7 0.4 %collective-permute-done.3.refs_6_ = f32[32,512]{1,0:T(8,128)S(1)} collective-permute-done((f32[32,512]{1,0:T(8,128)S(1)}, f32[32,512]{1,0:T(8,128)S(1)}, u32[]{:S(2)}, u32[]{:S(2)}) %collective-permute-start.3) | collective-permute-done | bytes 65568 | tf_op jit(solution)/shard_map/ppermute | solution.py:87
  16.1 0.0 collective-permute-done.4.refs_3_
  16.1 1.9 %collective-permute-start.5 = (f32[32,512]{1,0:T(8,128)S(1)}, f32[32,512]{1,0:T(8,128)S(1)}, u32[]{:S(2)}, u32[]{:S(2)}) collective-permute-start(f32[32,512]{1,0:T(8,128)S(1)} %collective-permute-done.3.refs_6_), channel_id=1, source_target_pairs={{0,4},{4,0},{8,12},{12,8},{16,20},{20,16},{24,28},{28,24},{1,5},{5... | collective-permute-start | bytes 196616 | tf_op jit(solution)/shard_map/ppermute | solution.py:87
  18.0 1.4 %collective-permute-done.2.refs_2_ = f32[64,512]{1,0:T(8,128)S(1)} collective-permute-done((f32[64,512]{1,0:T(8,128)S(1)}, f32[64,512]{1,0:T(8,128)S(1)}, u32[]{:S(2)}, u32[]{:S(2)}) %collective-permute-start.2) | collective-permute-done | bytes 131104 | tf_op jit(solution)/shard_map/ppermute | solution.py:87
  19.5 0.8 %collective-permute-done.7.refs_8_ = f32[64,512]{1,0:T(8,128)S(1)} collective-permute-done((f32[64,512]{1,0:T(8,128)S(1)}, f32[64,512]{1,0:T(8,128)S(1)}, u32[]{:S(2)}, u32[]{:S(2)}) %collective-permute-start.7) | collective-permute-done | bytes 131104 | tf_op jit(solution)/shard_map/ppermute | solution.py:87
  20.3 0.3 collective-permute-done.5.refs_5_
  20.5 0.0 copy-done
  20.6 0.9 %shard_map.39 = (f32[128,512]{1,0:T(8,128)S(1)}, f32[128,512]{1,0:T(8,128)S(1)}) custom-call(bf16[256,512]{1,0:T(8,128)(2,1)S(1)} %get-tuple-element.66.pick_ref, bf16[1536,512]{1,0:T(8,128)(2,1)S(1)} %get-tuple-element.14.right_ref, f32[64,512]{1,0:T(8,128)S(1)} %copy-done, f32[64,512]{1,0:T(8,128)S(1)} %collective-permute-done.refs_1_, ...), custom_call_target="tpu_custom_call" | custom-call | flops 671088640 | bytes 4194304 | tf_op jit(solution)/shard_map/pallas_call | solution.py:69
  21.4 0.1 collective-permute-start.9
  21.5 0.9 %shard_map.38 = (f32[128,512]{1,0:T(8,128)S(1)}, f32[128,512]{1,0:T(8,128)S(1)}) custom-call(bf16[256,512]{1,0:T(8,128)(2,1)S(1)} %get-tuple-element.65.pick_ref, bf16[1536,512]{1,0:T(8,128)(2,1)S(1)} %get-tuple-element.14.right_ref, f32[64,512]{1,0:T(8,128)S(1)} %copy-done, f32[64,512]{1,0:T(8,128)S(1)} %collective-permute-done.refs_1_, ...), custom_call_target="tpu_custom_call" | custom-call | flops 671088640 | bytes 4194304 | tf_op jit(solution)/shard_map/pallas_call | solution.py:69
  22.4 0.6 %collective-permute-start.8 = (f32[128,512]{1,0:T(8,128)S(1)}, f32[128,512]{1,0:T(8,128)S(1)}, u32[]{:S(2)}, u32[]{:S(2)}) collective-permute-start(f32[128,512]{1,0:T(8,128)S(1)} %get-tuple-element.18), channel_id=1, source_target_pairs={{0,1},{1,0},{2,3},{3,2},{4,5},{5,4},{6,7},{7,6},{8,9},{9,8},{10,11... | collective-permute-start | bytes 786440 | tf_op jit(solution)/shard_map/ppermute | solution.py:87
  22.9 0.1 collective-permute-done.9
  23.1 1.6 %collective-permute-start.10 = (f32[128,512]{1,0:T(8,128)S(1)}, f32[128,512]{1,0:T(8,128)S(1)}, u32[]{:S(2)}, u32[]{:S(2)}) collective-permute-start(f32[128,512]{1,0:T(8,128)S(1)} %add.22), channel_id=1, source_target_pairs={{0,2},{1,3},{2,0},{3,1},{4,6},{5,7},{6,4},{7,5},{8,10},{9,11},{10,... | collective-permute-start | bytes 786440 | tf_op jit(solution)/shard_map/ppermute | solution.py:87
  24.6 0.0 collective-permute-done.8
  24.6 6.9 %collective-permute-done.10 = f32[128,512]{1,0:T(8,128)S(1)} collective-permute-done((f32[128,512]{1,0:T(8,128)S(1)}, f32[128,512]{1,0:T(8,128)S(1)}, u32[]{:S(2)}, u32[]{:S(2)}) %collective-permute-start.10) | collective-permute-done | bytes 262176 | tf_op jit(solution)/shard_map/ppermute | solution.py:87
  31.5 0.8 %add_add_fusion = f32[128,512]{1,0:T(8,128)} fusion(f32[128,512]{1,0:T(8,128)S(1)} %collective-permute-done.10, f32[128,512]{1,0:T(8,128)S(1)} %get-tuple-element.17, f32[128,512]{1,0:T(8,128)S(1)} %collective-permute-done.8), kind=kLoop, calls=%fused_computation | loop fusion | flops 131072 | bytes 1048576 | tf_op jit(solution)/shard_map/add | solution.py:137
  (6 shorter events, 0.1 us)
Async XLA Ops:
  0.0 8.8 %collective-permute-start = (f32[64,512]{1,0:T(8,128)}, f32[64,512]{1,0:T(8,128)S(1)}, u32[]{:S(2)}, u32[]{:S(2)}) collective-permute-start(f32[64,512]{1,0:T(8,128)} %refs_0_.3), channel_id=1, source_target_pairs={{0,8},{4,12},{8,0},{12,4},{16,24},{20,28},{24,16},{28,20},{1,9},{5... | collective-permute-start | bytes 393224 | tf_op jit(solution)/shard_map/ppermute | solution.py:87
  3.0 11.2 %collective-permute-start.1 = (f32[64,512]{1,0:T(8,128)}, f32[64,512]{1,0:T(8,128)S(1)}, u32[]{:S(2)}, u32[]{:S(2)}) collective-permute-start(f32[64,512]{1,0:T(8,128)} %refs_0_.3), channel_id=1, source_target_pairs={{0,24},{4,28},{8,16},{12,20},{16,8},{20,12},{24,0},{28,4},{1,25},{... | collective-permute-start | bytes 393224 | tf_op jit(solution)/shard_map/ppermute | solution.py:87
  5.5 5.8 %collective-permute-start.6 = (f32[64,512]{1,0:T(8,128)}, f32[64,512]{1,0:T(8,128)S(1)}, u32[]{:S(2)}, u32[]{:S(2)}) collective-permute-start(f32[64,512]{1,0:T(8,128)} %refs_0_.3), channel_id=1, source_target_pairs={{0,4},{4,0},{8,12},{12,8},{16,20},{20,16},{24,28},{28,24},{1,5},{5... | collective-permute-start | bytes 393224 | tf_op jit(solution)/shard_map/ppermute | solution.py:87
  7.9 12.6 %copy-start = (f32[64,512]{1,0:T(8,128)S(1)}, f32[64,512]{1,0:T(8,128)}, u32[]{:S(2)}) copy-start(f32[64,512]{1,0:T(8,128)} %refs_0_.3) | copy-start | bytes 393220
  7.9 8.2 %collective-permute-start.3 = (f32[32,512]{1,0:T(8,128)S(1)}, f32[32,512]{1,0:T(8,128)S(1)}, u32[]{:S(2)}, u32[]{:S(2)}) collective-permute-start(f32[32,512]{1,0:T(8,128)S(1)} %get-tuple-element.68), channel_id=1, source_target_pairs={{0,16},{4,20},{8,24},{12,28},{16,0},{20,4},{24,8},{28,12},{1,17},{... | collective-permute-start | bytes 196616 | tf_op jit(solution)/shard_map/ppermute | solution.py:87
  8.8 7.2 %collective-permute-start.4 = (f32[64,512]{1,0:T(8,128)S(1)}, f32[64,512]{1,0:T(8,128)S(1)}, u32[]{:S(2)}, u32[]{:S(2)}) collective-permute-start(f32[64,512]{1,0:T(8,128)S(1)} %collective-permute-done.refs_1_), channel_id=1, source_target_pairs={{0,4},{4,0},{8,12},{12,8},{16,20},{20,16},{24,28},{28,24},{1,5},{5... | collective-permute-start | bytes 393224 | tf_op jit(solution)/shard_map/ppermute | solution.py:87
  9.6 1.2 %copy-start.1 = (f32[512,512]{1,0:T(8,128)S(1)}, f32[512,512]{1,0:T(8,128)}, u32[]{:S(2)}) copy-start(f32[512,512]{1,0:T(8,128)} %x_ref.1) | copy-start | bytes 3145732
  11.3 9.0 %collective-permute-start.7 = (f32[64,512]{1,0:T(8,128)S(1)}, f32[64,512]{1,0:T(8,128)S(1)}, u32[]{:S(2)}, u32[]{:S(2)}) collective-permute-start(f32[64,512]{1,0:T(8,128)S(1)} %pad_maximum_fusion), channel_id=1, source_target_pairs={{0,16},{4,20},{8,24},{12,28},{16,0},{20,4},{24,8},{28,12},{1,17},{... | collective-permute-start | bytes 393224 | tf_op jit(solution)/shard_map/ppermute | solution.py:87
  14.2 5.3 %collective-permute-start.2 = (f32[64,512]{1,0:T(8,128)S(1)}, f32[64,512]{1,0:T(8,128)S(1)}, u32[]{:S(2)}, u32[]{:S(2)}) collective-permute-start(f32[64,512]{1,0:T(8,128)S(1)} %collective-permute-done.1.refs_4_), channel_id=1, source_target_pairs={{0,4},{4,0},{8,12},{12,8},{16,20},{20,16},{24,28},{28,24},{1,5},{5... | collective-permute-start | bytes 393224 | tf_op jit(solution)/shard_map/ppermute | solution.py:87
  16.1 4.5 %collective-permute-start.5 = (f32[32,512]{1,0:T(8,128)S(1)}, f32[32,512]{1,0:T(8,128)S(1)}, u32[]{:S(2)}, u32[]{:S(2)}) collective-permute-start(f32[32,512]{1,0:T(8,128)S(1)} %collective-permute-done.3.refs_6_), channel_id=1, source_target_pairs={{0,4},{4,0},{8,12},{12,8},{16,20},{20,16},{24,28},{28,24},{1,5},{5... | collective-permute-start | bytes 196616 | tf_op jit(solution)/shard_map/ppermute | solution.py:87
  21.4 1.6 %collective-permute-start.9 = (f32[128,512]{1,0:T(8,128)S(1)}, f32[128,512]{1,0:T(8,128)S(1)}, u32[]{:S(2)}, u32[]{:S(2)}) collective-permute-start(f32[128,512]{1,0:T(8,128)S(1)} %get-tuple-element.20), channel_id=1, source_target_pairs={{0,1},{1,0},{2,3},{3,2},{4,5},{5,4},{6,7},{7,6},{8,9},{9,8},{10,11... | collective-permute-start | bytes 786440 | tf_op jit(solution)/shard_map/ppermute | solution.py:87
  22.4 2.2 %collective-permute-start.8 = (f32[128,512]{1,0:T(8,128)S(1)}, f32[128,512]{1,0:T(8,128)S(1)}, u32[]{:S(2)}, u32[]{:S(2)}) collective-permute-start(f32[128,512]{1,0:T(8,128)S(1)} %get-tuple-element.18), channel_id=1, source_target_pairs={{0,1},{1,0},{2,3},{3,2},{4,5},{5,4},{6,7},{7,6},{8,9},{9,8},{10,11... | collective-permute-start | bytes 786440 | tf_op jit(solution)/shard_map/ppermute | solution.py:87
  23.1 8.4 %collective-permute-start.10 = (f32[128,512]{1,0:T(8,128)S(1)}, f32[128,512]{1,0:T(8,128)S(1)}, u32[]{:S(2)}, u32[]{:S(2)}) collective-permute-start(f32[128,512]{1,0:T(8,128)S(1)} %add.22), channel_id=1, source_target_pairs={{0,2},{1,3},{2,0},{3,1},{4,6},{5,7},{6,4},{7,5},{8,10},{9,11},{10,... | collective-permute-start | bytes 786440 | tf_op jit(solution)/shard_map/ppermute | solution.py:87

commit v3 on v0

v3 whole, which is shorter than its diff:
```python
import functools

import jax
import jax.numpy as jnp
from jax import lax
from jax.experimental import pallas as pl
from jax.experimental.pallas import tpu as pltpu
from jax.sharding import PartitionSpec as P

MIB = 1024 * 1024
PARAMS = pltpu.CompilerParams(vmem_limit_bytes=8 * MIB)


def halves(x):
    high = x.astype(jnp.bfloat16)
    low = (x - high.astype(jnp.float32)).astype(jnp.bfloat16)
    return high, low


def times(left, right):
    return lax.dot_general(left, right, (((1,), (0,)), ((), ())), preferred_element_type=jnp.float32)


def cost(flops):
    return pl.CostEstimate(flops=flops, bytes_accessed=4 * MIB, transcendentals=0)


def prepare_kernel(x_ref, place_ref, right_ref, early_ref, late_ref):
    high, low = halves(x_ref[...].T)
    depth = high.shape[0]
    right_ref[:depth, :] = high
    right_ref[depth : 2 * depth, :] = high
    right_ref[2 * depth :, :] = low
    start = 0
    for ref in (early_ref, late_ref):
        column = lax.broadcasted_iota(jnp.int32, ref.shape, 1) + start
        ref[...] = jnp.where(column == place_ref[...], 1.0, 0.0).astype(jnp.bfloat16)
        start += ref.shape[1]


def prepare(amplitudes, place, early, late):
    width, depth = amplitudes.shape
    shapes = ((3 * depth, width), (place.shape[0], early), (place.shape[0], late))
    return pl.pallas_call(
        prepare_kernel,
        out_shape=[jax.ShapeDtypeStruct(shape, jnp.bfloat16) for shape in shapes],
        compiler_params=PARAMS,
        cost_estimate=cost(0),
    )(amplitudes, place)


def stack(pieces, parts):
    depth, start = pieces[0].shape[1], 0
    for piece in pieces:
        high, low = halves(piece[...])
        stop = start + piece.shape[0]
        parts[start:stop, :depth] = high
        parts[start:stop, depth:] = low
        start = stop


def choose_kernel(pick_ref, *refs):
    *pieces, out_ref, parts = refs
    stack(pieces, parts)
    out_ref[...] = times(pick_ref[...], parts[...]).astype(jnp.bfloat16)


def choose(pick, pieces):
    n, stacked = pick.shape
    depth = pieces[0].shape[1]
    return pl.pallas_call(
        choose_kernel,
        out_shape=jax.ShapeDtypeStruct((n, 2 * depth), jnp.bfloat16),
        scratch_shapes=[pltpu.VMEM((stacked, 2 * depth), jnp.bfloat16)],
        compiler_params=PARAMS,
        cost_estimate=cost(4 * n * stacked * depth),
    )(pick, *pieces)


def product_kernel(start, pieces_count, chosen_ref, pick_ref, right_ref, *refs):
    pieces = refs[:pieces_count]
    *outs, parts, left = refs[pieces_count:]
    stack(pieces, parts)
    n = left.shape[0]
    chosen = times(pick_ref[start : start + n, :], parts[...]) + chosen_ref[start : start + n, :].astype(jnp.float32)
    chosen = chosen.astype(jnp.bfloat16)
    depth = left.shape[1] // 3
    left[:, : 2 * depth] = chosen
    left[:, 2 * depth :] = chosen[:, :depth]
    total = times(left[...], right_ref[...])
    share = n // len(outs)
    for i, out in enumerate(outs):
        out[...] = total[i * share : (i + 1) * share]


def product(chosen, pick, right, pieces, start, share, count):
    depth, width = pieces[0].shape[1], right.shape[1]
    n = share * count
    return pl.pallas_call(
        functools.partial(product_kernel, start, len(pieces)),
        out_shape=[jax.ShapeDtypeStruct((share, width), jnp.float32)] * count,
        scratch_shapes=[
            pltpu.VMEM((pick.shape[1], 2 * depth), jnp.bfloat16),
            pltpu.VMEM((n, 3 * depth), jnp.bfloat16),
        ],
        compiler_params=PARAMS,
        cost_estimate=cost(2 * n * depth * (3 * width + 2 * pick.shape[1])),
    )(chosen, pick, right, *pieces)


def solution(mesh):
    rows, cols = mesh.shape["row"], mesh.shape["col"]

    def along(axis, size, m, x):
        return lax.ppermute(x, axis, [(i, i ^ m) for i in range(size)])

    def on_device(amplitudes, integrals, owner_order):
        height = integrals.shape[0]
        stacked = rows * height
        me, mine = lax.axis_index("row"), lax.axis_index("col")

        far = rows // 2
        cut = height // 32 * 16 or height
        rest = height - cut
        near, wide = range(2, far, 2), range(far + 2, rows, 2)

        straight = [*near, 0, *wide, 1]
        forwarded = [m + 1 for m in (*near, *wide)]
        upper, lower = [0] * rows, [0] * rows
        at = 0
        for m in straight:
            upper[m], lower[m] = at, at + cut
            at += height
        upper[far] = at
        early = at = at + cut
        lower[far], lower[far + 1] = at, at + rest
        at += 2 * rest
        for m in forwarded:
            upper[m], lower[m] = at, at + cut
            at += height
        upper[far + 1] = at

        block, row = (owner_order // height) ^ me, owner_order % height
        place = row
        for m in range(rows):
            place = place + jnp.where(block == m, jnp.where(row < cut, upper[m], lower[m] - cut), 0)
        share = stacked // cols
        place = place.reshape(cols, share)
        place = jnp.concatenate([jnp.take(place, mine ^ m, axis=0, mode="clip") for m in range(cols - 1, -1, -1)])
        prepared = prepare(amplitudes, place.reshape(stacked, 1), early, stacked - early)

        got = {0: integrals}
        got[1] = along("row", rows, 1, integrals)
        for m in wide:
            got[m] = along("row", rows, m, integrals)
        top = along("row", rows, far, integrals[:cut])
        for m in near:
            got[m] = along("row", rows, m, integrals)
        for m in near:
            got[m + 1] = along("row", rows, 1, got[m])
        to_forward, right, pick_early, pick_late = lax.optimization_barrier((top, *prepared))
        top_next = along("row", rows, 1, to_forward)
        below = []
        if rest:
            below.append(along("row", rows, far, jnp.concatenate([integrals[cut:], got[1][cut:]])))
        for m in wide:
            got[m + 1] = along("row", rows, 1, got[m])
        first = [*[got[m] for m in straight], top]
        last = [*below, *[got[m] for m in forwarded], top_next]
        if height % 16:
            first, last = [jnp.concatenate(first)], [jnp.concatenate(last)]
        chosen = choose(pick_early, first)

        def sums(start, count):
            return product(chosen, pick_late, right, last, start * share, share, count)

        moved = []
        for t in range(0, cols - 2, 2):
            (other,) = sums(t, 1)
            own, *home = sums(t + 1, 3 if t == cols - 4 else 1)
            moved.append(along("col", cols, cols - 2 - t, own + along("col", cols, 1, other)))
        other, own = home if moved else sums(0, 2)
        out = own + along("col", cols, 1, other)
        for x in moved:
            out = out + x
        return out

    in_specs = (P("row", "col"), P("row", "col"), P())
    out_specs = P("col", "row")
    return jax.shard_map(
        on_device, mesh=mesh, in_specs=in_specs, out_specs=out_specs, check_vma=False
    )
```

time: 89 us -> 32.2 us (0.36)
  waiting for transfers between devices: 69.6 us -> 11.3 us
  starting transfers between devices: 0.04 us -> 14.1 us
  between operations: 13.4 us -> 0.1 us
  matrix products: 3.08 us -> 0 us
  Pallas kernels: 0 us -> 2.67 us
    all_gather x1 -> x0, waiting for transfers between devices: 45 us -> none  [on_device(): lax.all_gather(integrals, 'row', axis=0, tiled=True)]
    reduce_scatter x1 -> x0, waiting for transfers between devices: 23.8 us -> none  [on_device(): return lax.psum_scatter(arranged, 'col', scatter_dimension=0, tiled=True)]
    ppermute x0 -> x11, starting transfers between devices: none -> 14.1 us  [along(): return lax.ppermute(x, axis, [(i, i ^ m) for i in range(size)])]
    ppermute x0 -> x11, waiting for transfers between devices: none -> 11.3 us  [along(): return lax.ppermute(x, axis, [(i, i ^ m) for i in range(size)])]
    dot_general x1 -> x0, matrix products: 3.08 us -> none  [contract(): lax.dot_general(left, right, (((1,), (1,)), ((), ())), precision=lax.Prec...]
    pallas_call x0 -> x4, Pallas kernels: none -> 2.67 us  [the longest x2 1.47 us: product(): pl.pallas_call(functools.partial(product_kernel, start, len(pieces)), out...]
    gather x1, local copies, waits for them, and re-layouts: 1.62 us -> 0.01 us  [on_device(): jnp.take(place, mine ^ m, axis=0, mode='clip')]
    unnamed x4, local copies, waits for them, and re-layouts: 0.01 us -> 1.23 us
  transfers between devices with their start and end apart: 2 -> 11, of which waited for: 2 -> 3; matrix products, arithmetic and copies ran while one was open for 0% -> 6% of each run, Pallas kernels for 0% -> 7%
where the time goes in v3:
time: 32.2 us; the launch traced here: 31.9 us
  starting transfers between devices  14.1 us (44%)
  waiting for transfers between devices  11.3 us (35%)
  Pallas kernels  2.67 us (8%)
  local copies, waits for them, and re-layouts  2.27 us (7%)
  other arithmetic  1.52 us (5%)
    ppermute x11, starting transfers between devices, along(): return lax.ppermute(x, axis, [(i, i ^ m) for i in range(size)])  14.1 us
    ppermute x11, waiting for transfers between devices, along(): return lax.ppermute(x, axis, [(i, i ^ m) for i in range(size)])  11.3 us
    pallas_call x2, Pallas kernels, product(): pl.pallas_call(functools.partial(product_kernel, start, len(pieces)), out...  1.47 us
    unnamed x4, local copies, waits for them, and re-layouts  1.23 us
    slice x1, local copies, waits for them, and re-layouts, on_device(): integrals[cut:]  0.88 us
    add x1, other arithmetic, on_device(): out = out + x  0.77 us
    pallas_call x1, Pallas kernels, choose(): pl.pallas_call(choose_kernel, out_shape=jax.ShapeDtypeStruct((n, 2 * dept...  0.71 us
    reshape x1, other arithmetic, on_device(): place = place.reshape(cols, share)  0.7 us
  transfers between devices with their start and end apart: 11, of which 3 were waited for; matrix products, arithmetic and copies ran while one was open for 6% of the time, Pallas kernels for 7%

profile of v3, /device:TPU:0, one launch (start us, length us, event | category | flops | bytes accessed | tf_op | source)
XLA Modules:
  0.0 31.9 jit_solution(12957527750961449116)
XLA Ops:
  0.0 0.0 copy-start.1
  0.0 5.0 %collective-permute-start.2 = (f32[64,512]{1,0:T(8,128)}, f32[64,512]{1,0:T(8,128)S(1)}, u32[]{:S(2)}, u32[]{:S(2)}) collective-permute-start(f32[64,512]{1,0:T(8,128)} %refs_1_.1), channel_id=1, source_target_pairs={{0,24},{4,28},{8,16},{12,20},{16,8},{20,12},{24,0},{28,4},{1,25},{... | collective-permute-start | bytes 393224 | tf_op jit(solution)/shard_map/ppermute | solution.py:115
  5.1 0.0 collective-permute-start.1
  5.1 1.5 %collective-permute-start.3 = (f32[64,512]{1,0:T(8,128)}, f32[64,512]{1,0:T(8,128)S(1)}, u32[]{:S(2)}, u32[]{:S(2)}) collective-permute-start(f32[64,512]{1,0:T(8,128)} %refs_1_.1), channel_id=1, source_target_pairs={{0,4},{4,0},{8,12},{12,8},{16,20},{20,16},{24,28},{28,24},{1,5},{5... | collective-permute-start | bytes 393224 | tf_op jit(solution)/shard_map/ppermute | solution.py:115
  6.6 0.9 %fusion.7 = (f32[32,512]{1,0:T(8,128)S(1)}, f32[32,512]{1,0:T(8,128)S(1)}) fusion(f32[64,512]{1,0:T(8,128)} %refs_1_.1), kind=kLoop, calls=%fused_computation.21 | loop fusion | bytes 262144 | tf_op jit(solution)/shard_map/slice | solution.py:165
  7.5 0.8 %collective-permute-start = (f32[32,512]{1,0:T(8,128)S(1)}, f32[32,512]{1,0:T(8,128)S(1)}, u32[]{:S(2)}, u32[]{:S(2)}) collective-permute-start(f32[32,512]{1,0:T(8,128)S(1)} %get-tuple-element.70), channel_id=1, source_target_pairs={{0,16},{4,20},{8,24},{12,28},{16,0},{20,4},{24,8},{28,12},{1,17},{... | collective-permute-start | bytes 196616 | tf_op jit(solution)/shard_map/ppermute | solution.py:115
  8.3 0.7 %add_bitcast_fusion = s32[4,128]{1,0:T(4,128)S(1)} fusion(s32[512]{0:T(512)} %param.5, s32[]{:T(128)S(6)} %axis_index.23), kind=kLoop, calls=%fused_computation.9 | loop fusion | flops 22016 | bytes 4100 | tf_op jit(solution)/shard_map/reshape | solution.py:148
  9.0 1.2 %collective-permute-done.3.refs_3_ = f32[64,512]{1,0:T(8,128)S(1)} collective-permute-done((f32[64,512]{1,0:T(8,128)}, f32[64,512]{1,0:T(8,128)S(1)}, u32[]{:S(2)}, u32[]{:S(2)}) %collective-permute-start.3) | collective-permute-done | bytes 131104 | tf_op jit(solution)/shard_map/ppermute | solution.py:115
  10.3 1.0 %collective-permute-start.4 = (f32[64,512]{1,0:T(8,128)S(1)}, f32[64,512]{1,0:T(8,128)S(1)}, u32[]{:S(2)}, u32[]{:S(2)}) collective-permute-start(f32[64,512]{1,0:T(8,128)S(1)} %pad_maximum_fusion), channel_id=1, source_target_pairs={{0,16},{4,20},{8,24},{12,28},{16,0},{20,4},{24,8},{28,12},{1,17},{... | collective-permute-start | bytes 393224 | tf_op jit(solution)/shard_map/ppermute | solution.py:115
  11.3 0.0 collective-permute-done.2.refs_2_
  11.3 1.3 %collective-permute-start.6 = (f32[64,512]{1,0:T(8,128)S(1)}, f32[64,512]{1,0:T(8,128)S(1)}, u32[]{:S(2)}, u32[]{:S(2)}) collective-permute-start(f32[64,512]{1,0:T(8,128)S(1)} %collective-permute-done.2.refs_2_), channel_id=1, source_target_pairs={{0,4},{4,0},{8,12},{12,8},{16,20},{20,16},{24,28},{28,24},{1,5},{5... | collective-permute-start | bytes 393224 | tf_op jit(solution)/shard_map/ppermute | solution.py:115
  12.6 0.0 collective-permute-done.1.refs_0_
  12.6 1.7 %collective-permute-start.5 = (f32[64,512]{1,0:T(8,128)S(1)}, f32[64,512]{1,0:T(8,128)S(1)}, u32[]{:S(2)}, u32[]{:S(2)}) collective-permute-start(f32[64,512]{1,0:T(8,128)S(1)} %collective-permute-done.1.refs_0_), channel_id=1, source_target_pairs={{0,4},{4,0},{8,12},{12,8},{16,20},{20,16},{24,28},{28,24},{1,5},{5... | collective-permute-start | bytes 393224 | tf_op jit(solution)/shard_map/ppermute | solution.py:115
  14.4 0.1 copy.4.place_ref
  14.5 0.0 copy-start
  14.6 1.2 %copy-done = f32[512,512]{1,0:T(8,128)S(1)} copy-done((f32[512,512]{1,0:T(8,128)S(1)}, f32[512,512]{1,0:T(8,128)}, u32[]{:S(2)}) %copy-start) | copy-done | bytes 1048600
  15.8 0.5 %shard_map.37 = (bf16[1536,512]{1,0:T(8,128)(2,1)S(1)}, bf16[512,288]{1,0:T(8,128)(2,1)S(1)}, bf16[512,224]{1,0:T(8,128)(2,1)S(1)}) custom-call(f32[512,512]{1,0:T(8,128)S(1)} %copy-done, s32[512,1]{1,0:T(8,128)S(1)} %copy.4.place_ref), custom_call_target="tpu_custom_call" | custom-call | bytes 4194304 | tf_op jit(solution)/shard_map/pallas_call | solution.py:44
  16.3 0.0 collective-permute-done.refs_4_
  16.3 0.3 %collective-permute-start.7 = (f32[32,512]{1,0:T(8,128)S(1)}, f32[32,512]{1,0:T(8,128)S(1)}, u32[]{:S(2)}, u32[]{:S(2)}) collective-permute-start(f32[32,512]{1,0:T(8,128)S(1)} %collective-permute-done.refs_4_), channel_id=1, source_target_pairs={{0,4},{4,0},{8,12},{12,8},{16,20},{20,16},{24,28},{28,24},{1,5},{5... | collective-permute-start | bytes 196616 | tf_op jit(solution)/shard_map/ppermute | solution.py:115
  16.6 0.0 copy-done.1
  16.6 0.7 %shard_map.38.chosen_ref = bf16[512,1024]{1,0:T(8,128)(2,1)S(1)} custom-call(bf16[512,288]{1,0:T(8,128)(2,1)S(1)} %get-tuple-element.18.pick_ref, f32[64,512]{1,0:T(8,128)S(1)} %collective-permute-done.1.refs_0_, f32[64,512]{1,0:T(8,128)S(1)} %copy-done.1, f32[64,512]{1,0:T(8,128)S(1)} %collective-permute-done.2.refs_2_, ...), custom_call_target="tpu_custom_call" | custom-call | flops 301989888 | bytes 4194304 | tf_op jit(solution)/shard_map/pallas_call | solution.py:71
  17.4 3.3 %collective-permute-done.7.refs_3_ = f32[32,512]{1,0:T(8,128)S(1)} collective-permute-done((f32[32,512]{1,0:T(8,128)S(1)}, f32[32,512]{1,0:T(8,128)S(1)}, u32[]{:S(2)}, u32[]{:S(2)}) %collective-permute-start.7) | collective-permute-done | bytes 65568 | tf_op jit(solution)/shard_map/ppermute | solution.py:115
  20.6 0.0 collective-permute-done.6.refs_2_
  20.6 0.0 collective-permute-done.5.refs_1_
  20.6 0.0 collective-permute-done.4.refs_0_
  20.6 0.5 %shard_map.40 = f32[128,512]{1,0:T(8,128)S(1)} custom-call(bf16[512,1024]{1,0:T(8,128)(2,1)S(1)} %shard_map.38.chosen_ref, bf16[512,224]{1,0:T(8,128)(2,1)S(1)} %get-tuple-element.19.pick_ref, bf16[1536,512]{1,0:T(8,128)(2,1)S(1)} %get-tuple-element.20.right_ref, f32[64,512]{1,0:T(8,128)S(1)} %collective-permute-done.4.refs_0_, ...), custom_call_target="tpu_custom_call" | custom-call | flops 260046848 | bytes 4194304 | tf_op jit(solution)/shard_map/pallas_call | solution.py:99
  21.1 0.1 collective-permute-start.9
  21.2 1.0 %shard_map.39 = (f32[128,512]{1,0:T(8,128)S(1)}, f32[128,512]{1,0:T(8,128)S(1)}, f32[128,512]{1,0:T(8,128)S(1)}) custom-call(bf16[512,1024]{1,0:T(8,128)(2,1)S(1)} %shard_map.38.chosen_ref, bf16[512,224]{1,0:T(8,128)(2,1)S(1)} %get-tuple-element.19.pick_ref, bf16[1536,512]{1,0:T(8,128)(2,1)S(1)} %get-tuple-element.20.right_ref, ...), custom_call_target="tpu_custom_call" | custom-call | flops 780140544 | bytes 4194304 | tf_op jit(solution)/shard_map/pallas_call | solution.py:99
  22.2 0.6 %collective-permute-start.8 = (f32[128,512]{1,0:T(8,128)S(1)}, f32[128,512]{1,0:T(8,128)S(1)}, u32[]{:S(2)}, u32[]{:S(2)}) collective-permute-start(f32[128,512]{1,0:T(8,128)S(1)} %get-tuple-element.23), channel_id=1, source_target_pairs={{0,1},{1,0},{2,3},{3,2},{4,5},{5,4},{6,7},{7,6},{8,9},{9,8},{10,11... | collective-permute-start | bytes 786440 | tf_op jit(solution)/shard_map/ppermute | solution.py:115
  22.7 0.0 collective-permute-done.9
  22.8 1.6 %collective-permute-start.10 = (f32[128,512]{1,0:T(8,128)S(1)}, f32[128,512]{1,0:T(8,128)S(1)}, u32[]{:S(2)}, u32[]{:S(2)}) collective-permute-start(f32[128,512]{1,0:T(8,128)S(1)} %add.47), channel_id=1, source_target_pairs={{0,2},{1,3},{2,0},{3,1},{4,6},{5,7},{6,4},{7,5},{8,10},{9,11},{10,... | collective-permute-start | bytes 786440 | tf_op jit(solution)/shard_map/ppermute | solution.py:115
  24.4 0.0 collective-permute-done.8
  24.4 6.8 %collective-permute-done.10 = f32[128,512]{1,0:T(8,128)S(1)} collective-permute-done((f32[128,512]{1,0:T(8,128)S(1)}, f32[128,512]{1,0:T(8,128)S(1)}, u32[]{:S(2)}, u32[]{:S(2)}) %collective-permute-start.10) | collective-permute-done | bytes 262176 | tf_op jit(solution)/shard_map/ppermute | solution.py:115
  31.2 0.8 %add_add_fusion = f32[128,512]{1,0:T(8,128)} fusion(f32[128,512]{1,0:T(8,128)S(1)} %collective-permute-done.10, f32[128,512]{1,0:T(8,128)S(1)} %get-tuple-element.22, f32[128,512]{1,0:T(8,128)S(1)} %collective-permute-done.8), kind=kLoop, calls=%fused_computation | loop fusion | flops 131072 | bytes 1048576 | tf_op jit(solution)/shard_map/add | solution.py:185
  (5 shorter events, 0.1 us)
Async XLA Ops:
  0.0 16.6 %copy-start.1 = (f32[64,512]{1,0:T(8,128)S(1)}, f32[64,512]{1,0:T(8,128)}, u32[]{:S(2)}) copy-start(f32[64,512]{1,0:T(8,128)} %refs_1_.1) | copy-start | bytes 393220
  0.0 11.3 %collective-permute-start.2 = (f32[64,512]{1,0:T(8,128)}, f32[64,512]{1,0:T(8,128)S(1)}, u32[]{:S(2)}, u32[]{:S(2)}) collective-permute-start(f32[64,512]{1,0:T(8,128)} %refs_1_.1), channel_id=1, source_target_pairs={{0,24},{4,28},{8,16},{12,20},{16,8},{20,12},{24,0},{28,4},{1,25},{... | collective-permute-start | bytes 393224 | tf_op jit(solution)/shard_map/ppermute | solution.py:115
  5.1 7.6 %collective-permute-start.1 = (f32[64,512]{1,0:T(8,128)}, f32[64,512]{1,0:T(8,128)S(1)}, u32[]{:S(2)}, u32[]{:S(2)}) collective-permute-start(f32[64,512]{1,0:T(8,128)} %refs_1_.1), channel_id=1, source_target_pairs={{0,8},{4,12},{8,0},{12,4},{16,24},{20,28},{24,16},{28,20},{1,9},{5... | collective-permute-start | bytes 393224 | tf_op jit(solution)/shard_map/ppermute | solution.py:115
  5.1 5.2 %collective-permute-start.3 = (f32[64,512]{1,0:T(8,128)}, f32[64,512]{1,0:T(8,128)S(1)}, u32[]{:S(2)}, u32[]{:S(2)}) collective-permute-start(f32[64,512]{1,0:T(8,128)} %refs_1_.1), channel_id=1, source_target_pairs={{0,4},{4,0},{8,12},{12,8},{16,20},{20,16},{24,28},{28,24},{1,5},{5... | collective-permute-start | bytes 393224 | tf_op jit(solution)/shard_map/ppermute | solution.py:115
  7.5 8.8 %collective-permute-start = (f32[32,512]{1,0:T(8,128)S(1)}, f32[32,512]{1,0:T(8,128)S(1)}, u32[]{:S(2)}, u32[]{:S(2)}) collective-permute-start(f32[32,512]{1,0:T(8,128)S(1)} %get-tuple-element.70), channel_id=1, source_target_pairs={{0,16},{4,20},{8,24},{12,28},{16,0},{20,4},{24,8},{28,12},{1,17},{... | collective-permute-start | bytes 196616 | tf_op jit(solution)/shard_map/ppermute | solution.py:115
  10.3 10.4 %collective-permute-start.4 = (f32[64,512]{1,0:T(8,128)S(1)}, f32[64,512]{1,0:T(8,128)S(1)}, u32[]{:S(2)}, u32[]{:S(2)}) collective-permute-start(f32[64,512]{1,0:T(8,128)S(1)} %pad_maximum_fusion), channel_id=1, source_target_pairs={{0,16},{4,20},{8,24},{12,28},{16,0},{20,4},{24,8},{28,12},{1,17},{... | collective-permute-start | bytes 393224 | tf_op jit(solution)/shard_map/ppermute | solution.py:115
  11.3 9.3 %collective-permute-start.6 = (f32[64,512]{1,0:T(8,128)S(1)}, f32[64,512]{1,0:T(8,128)S(1)}, u32[]{:S(2)}, u32[]{:S(2)}) collective-permute-start(f32[64,512]{1,0:T(8,128)S(1)} %collective-permute-done.2.refs_2_), channel_id=1, source_target_pairs={{0,4},{4,0},{8,12},{12,8},{16,20},{20,16},{24,28},{28,24},{1,5},{5... | collective-permute-start | bytes 393224 | tf_op jit(solution)/shard_map/ppermute | solution.py:115
  12.6 8.0 %collective-permute-start.5 = (f32[64,512]{1,0:T(8,128)S(1)}, f32[64,512]{1,0:T(8,128)S(1)}, u32[]{:S(2)}, u32[]{:S(2)}) collective-permute-start(f32[64,512]{1,0:T(8,128)S(1)} %collective-permute-done.1.refs_0_), channel_id=1, source_target_pairs={{0,4},{4,0},{8,12},{12,8},{16,20},{20,16},{24,28},{28,24},{1,5},{5... | collective-permute-start | bytes 393224 | tf_op jit(solution)/shard_map/ppermute | solution.py:115
  14.5 1.2 %copy-start = (f32[512,512]{1,0:T(8,128)S(1)}, f32[512,512]{1,0:T(8,128)}, u32[]{:S(2)}) copy-start(f32[512,512]{1,0:T(8,128)} %x_ref.1) | copy-start | bytes 3145732
  16.3 4.3 %collective-permute-start.7 = (f32[32,512]{1,0:T(8,128)S(1)}, f32[32,512]{1,0:T(8,128)S(1)}, u32[]{:S(2)}, u32[]{:S(2)}) collective-permute-start(f32[32,512]{1,0:T(8,128)S(1)} %collective-permute-done.refs_4_), channel_id=1, source_target_pairs={{0,4},{4,0},{8,12},{12,8},{16,20},{20,16},{24,28},{28,24},{1,5},{5... | collective-permute-start | bytes 196616 | tf_op jit(solution)/shard_map/ppermute | solution.py:115
  21.1 1.6 %collective-permute-start.9 = (f32[128,512]{1,0:T(8,128)S(1)}, f32[128,512]{1,0:T(8,128)S(1)}, u32[]{:S(2)}, u32[]{:S(2)}) collective-permute-start(f32[128,512]{1,0:T(8,128)S(1)} %shard_map.40), channel_id=1, source_target_pairs={{0,1},{1,0},{2,3},{3,2},{4,5},{5,4},{6,7},{7,6},{8,9},{9,8},{10,11... | collective-permute-start | bytes 786440 | tf_op jit(solution)/shard_map/ppermute | solution.py:115
  22.2 2.2 %collective-permute-start.8 = (f32[128,512]{1,0:T(8,128)S(1)}, f32[128,512]{1,0:T(8,128)S(1)}, u32[]{:S(2)}, u32[]{:S(2)}) collective-permute-start(f32[128,512]{1,0:T(8,128)S(1)} %get-tuple-element.23), channel_id=1, source_target_pairs={{0,1},{1,0},{2,3},{3,2},{4,5},{5,4},{6,7},{7,6},{8,9},{9,8},{10,11... | collective-permute-start | bytes 786440 | tf_op jit(solution)/shard_map/ppermute | solution.py:115
  22.8 8.4 %collective-permute-start.10 = (f32[128,512]{1,0:T(8,128)S(1)}, f32[128,512]{1,0:T(8,128)S(1)}, u32[]{:S(2)}, u32[]{:S(2)}) collective-permute-start(f32[128,512]{1,0:T(8,128)S(1)} %add.47), channel_id=1, source_target_pairs={{0,2},{1,3},{2,0},{3,1},{4,6},{5,7},{6,4},{7,5},{8,10},{9,11},{10,... | collective-permute-start | bytes 786440 | tf_op jit(solution)/shard_map/ppermute | solution.py:115

commit v4 on v3

--- a/solution.py
+++ b/solution.py
@@ -25,12 +25,25 @@
     return pl.CostEstimate(flops=flops, bytes_accessed=4 * MIB, transcendentals=0)
 
 
-def prepare_kernel(x_ref, place_ref, right_ref, early_ref, late_ref):
+def lay_out_kernel(x_ref, right_ref):
     high, low = halves(x_ref[...].T)
     depth = high.shape[0]
     right_ref[:depth, :] = high
     right_ref[depth : 2 * depth, :] = high
     right_ref[2 * depth :, :] = low
+
+
+def lay_out(amplitudes):
+    width, depth = amplitudes.shape
+    return pl.pallas_call(
+        lay_out_kernel,
+        out_shape=jax.ShapeDtypeStruct((3 * depth, width), jnp.bfloat16),
+        compiler_params=PARAMS,
+        cost_estimate=cost(0),
+    )(amplitudes)
+
+
+def name_kernel(place_ref, early_ref, late_ref):
     start = 0
     for ref in (early_ref, late_ref):
         column = lax.broadcasted_iota(jnp.int32, ref.shape, 1) + start
@@ -38,15 +51,14 @@
         start += ref.shape[1]
 
 
-def prepare(amplitudes, place, early, late):
-    width, depth = amplitudes.shape
-    shapes = ((3 * depth, width), (place.shape[0], early), (place.shape[0], late))
-    return pl.pallas_call(
-        prepare_kernel,
-        out_shape=[jax.ShapeDtypeStruct(shape, jnp.bfloat16) for shape in shapes],
+def name_rows(place, early, late):
+    n = place.shape[0]
+    return pl.pallas_call(
+        name_kernel,
+        out_shape=[jax.ShapeDtypeStruct((n, width), jnp.bfloat16) for width in (early, late)],
         compiler_params=PARAMS,
         cost_estimate=cost(0),
-    )(amplitudes, place)
+    )(place)
 
 
 def stack(pieces, parts):
@@ -147,7 +159,8 @@
         share = stacked // cols
         place = place.reshape(cols, share)
         place = jnp.concatenate([jnp.take(place, mine ^ m, axis=0, mode="clip") for m in range(cols - 1, -1, -1)])
-        prepared = prepare(amplitudes, place.reshape(stacked, 1), early, stacked - early)
+        right = lay_out(amplitudes)
+        picks = name_rows(place.reshape(stacked, 1), early, stacked - early)
 
         got = {0: integrals}
         got[1] = along("row", rows, 1, integrals)
@@ -158,7 +171,7 @@
             got[m] = along("row", rows, m, integrals)
         for m in near:
             got[m + 1] = along("row", rows, 1, got[m])
-        to_forward, right, pick_early, pick_late = lax.optimization_barrier((top, *prepared))
+        to_forward, pick_early, pick_late = lax.optimization_barrier((top, *picks))
         top_next = along("row", rows, 1, to_forward)
         below = []
         if rest:

time: 32.2 us -> 31.8 us (0.988)
  local copies, waits for them, and re-layouts: 2.27 us -> 1.05 us
  waiting for transfers between devices: 11.3 us -> 12 us
    unnamed x4, local copies, waits for them, and re-layouts: 1.23 us -> 0.01 us
    ppermute x11, waiting for transfers between devices: 11.3 us -> 12 us  [along(): return lax.ppermute(x, axis, [(i, i ^ m) for i in range(size)])]
where the time goes in v4:
time: 31.8 us; the launch traced here: 31.6 us
  starting transfers between devices  14.2 us (45%)
  waiting for transfers between devices  12 us (38%)
  Pallas kernels  2.73 us (9%)
  other arithmetic  1.52 us (5%)
  local copies, waits for them, and re-layouts  1.05 us (3%)
    ppermute x11, starting transfers between devices, along(): return lax.ppermute(x, axis, [(i, i ^ m) for i in range(size)])  14.2 us
    ppermute x11, waiting for transfers between devices, along(): return lax.ppermute(x, axis, [(i, i ^ m) for i in range(size)])  12 us
    pallas_call x2, Pallas kernels, product(): pl.pallas_call(functools.partial(product_kernel, start, len(pieces)), out...  1.47 us
    slice x1, local copies, waits for them, and re-layouts, on_device(): integrals[cut:]  0.88 us
    add x1, other arithmetic, on_device(): out = out + x  0.77 us
    pallas_call x1, Pallas kernels, choose(): pl.pallas_call(choose_kernel, out_shape=jax.ShapeDtypeStruct((n, 2 * dept...  0.71 us
    reshape x1, other arithmetic, on_device(): place = place.reshape(cols, share)  0.7 us
  transfers between devices with their start and end apart: 11, of which 3 were waited for; matrix products, arithmetic and copies ran while one was open for 6% of the time, Pallas kernels for 7%

profile of v4, /device:TPU:0, one launch (start us, length us, event | category | flops | bytes accessed | tf_op | source)
XLA Modules:
  0.0 31.6 jit_solution(1169590404899662669)
XLA Ops:
  0.0 0.0 copy-start
  0.0 5.0 %collective-permute-start.2 = (f32[64,512]{1,0:T(8,128)}, f32[64,512]{1,0:T(8,128)S(1)}, u32[]{:S(2)}, u32[]{:S(2)}) collective-permute-start(f32[64,512]{1,0:T(8,128)} %refs_1_.1), channel_id=1, source_target_pairs={{0,24},{4,28},{8,16},{12,20},{16,8},{20,12},{24,0},{28,4},{1,25},{... | collective-permute-start | bytes 393224 | tf_op jit(solution)/shard_map/ppermute | solution.py:127
  5.1 0.0 collective-permute-start.1
  5.1 1.5 %collective-permute-start.3 = (f32[64,512]{1,0:T(8,128)}, f32[64,512]{1,0:T(8,128)S(1)}, u32[]{:S(2)}, u32[]{:S(2)}) collective-permute-start(f32[64,512]{1,0:T(8,128)} %refs_1_.1), channel_id=1, source_target_pairs={{0,4},{4,0},{8,12},{12,8},{16,20},{20,16},{24,28},{28,24},{1,5},{5... | collective-permute-start | bytes 393224 | tf_op jit(solution)/shard_map/ppermute | solution.py:127
  6.6 0.9 %fusion.7 = (f32[32,512]{1,0:T(8,128)S(1)}, f32[32,512]{1,0:T(8,128)S(1)}) fusion(f32[64,512]{1,0:T(8,128)} %refs_1_.1), kind=kLoop, calls=%fused_computation.21 | loop fusion | bytes 262144 | tf_op jit(solution)/shard_map/slice | solution.py:178
  7.5 0.8 %collective-permute-start = (f32[32,512]{1,0:T(8,128)S(1)}, f32[32,512]{1,0:T(8,128)S(1)}, u32[]{:S(2)}, u32[]{:S(2)}) collective-permute-start(f32[32,512]{1,0:T(8,128)S(1)} %get-tuple-element.66), channel_id=1, source_target_pairs={{0,16},{4,20},{8,24},{12,28},{16,0},{20,4},{24,8},{28,12},{1,17},{... | collective-permute-start | bytes 196616 | tf_op jit(solution)/shard_map/ppermute | solution.py:127
  8.3 0.7 %add_bitcast_fusion = s32[4,128]{1,0:T(4,128)S(1)} fusion(s32[512]{0:T(512)} %param.5, s32[]{:T(128)S(6)} %axis_index.23), kind=kLoop, calls=%fused_computation.9 | loop fusion | flops 22016 | bytes 4100 | tf_op jit(solution)/shard_map/reshape | solution.py:160
  9.0 1.2 %collective-permute-done.3.refs_3_ = f32[64,512]{1,0:T(8,128)S(1)} collective-permute-done((f32[64,512]{1,0:T(8,128)}, f32[64,512]{1,0:T(8,128)S(1)}, u32[]{:S(2)}, u32[]{:S(2)}) %collective-permute-start.3) | collective-permute-done | bytes 131104 | tf_op jit(solution)/shard_map/ppermute | solution.py:127
  10.3 1.0 %collective-permute-start.4 = (f32[64,512]{1,0:T(8,128)S(1)}, f32[64,512]{1,0:T(8,128)S(1)}, u32[]{:S(2)}, u32[]{:S(2)}) collective-permute-start(f32[64,512]{1,0:T(8,128)S(1)} %pad_maximum_fusion), channel_id=1, source_target_pairs={{0,16},{4,20},{8,24},{12,28},{16,0},{20,4},{24,8},{28,12},{1,17},{... | collective-permute-start | bytes 393224 | tf_op jit(solution)/shard_map/ppermute | solution.py:127
  11.3 0.0 collective-permute-done.2.refs_2_
  11.3 1.3 %collective-permute-start.6 = (f32[64,512]{1,0:T(8,128)S(1)}, f32[64,512]{1,0:T(8,128)S(1)}, u32[]{:S(2)}, u32[]{:S(2)}) collective-permute-start(f32[64,512]{1,0:T(8,128)S(1)} %collective-permute-done.2.refs_2_), channel_id=1, source_target_pairs={{0,4},{4,0},{8,12},{12,8},{16,20},{20,16},{24,28},{28,24},{1,5},{5... | collective-permute-start | bytes 393224 | tf_op jit(solution)/shard_map/ppermute | solution.py:127
  12.6 0.0 collective-permute-done.1.refs_0_
  12.6 1.7 %collective-permute-start.5 = (f32[64,512]{1,0:T(8,128)S(1)}, f32[64,512]{1,0:T(8,128)S(1)}, u32[]{:S(2)}, u32[]{:S(2)}) collective-permute-start(f32[64,512]{1,0:T(8,128)S(1)} %collective-permute-done.1.refs_0_), channel_id=1, source_target_pairs={{0,4},{4,0},{8,12},{12,8},{16,20},{20,16},{24,28},{28,24},{1,5},{5... | collective-permute-start | bytes 393224 | tf_op jit(solution)/shard_map/ppermute | solution.py:127
  14.3 0.0 copy-start.1
  14.3 0.1 copy.4.place_ref
  14.5 0.2 shard_map.37
  14.7 0.0 collective-permute-done.refs_4_
  14.7 0.6 %collective-permute-start.7 = (f32[32,512]{1,0:T(8,128)S(1)}, f32[32,512]{1,0:T(8,128)S(1)}, u32[]{:S(2)}, u32[]{:S(2)}) collective-permute-start(f32[32,512]{1,0:T(8,128)S(1)} %collective-permute-done.refs_4_), channel_id=1, source_target_pairs={{0,4},{4,0},{8,12},{12,8},{16,20},{20,16},{24,28},{28,24},{1,5},{5... | collective-permute-start | bytes 196616 | tf_op jit(solution)/shard_map/ppermute | solution.py:127
  15.3 0.0 copy-done
  15.3 0.3 %shard_map.39.right_ref = bf16[1536,512]{1,0:T(8,128)(2,1)S(1)} custom-call(f32[512,512]{1,0:T(8,128)S(1)} %copy-done), custom_call_target="tpu_custom_call" | custom-call | bytes 4194304 | tf_op jit(solution)/shard_map/pallas_call | solution.py:38
  15.7 0.0 copy-done.1
  15.7 0.7 %shard_map.38.chosen_ref = bf16[512,1024]{1,0:T(8,128)(2,1)S(1)} custom-call(bf16[512,288]{1,0:T(8,128)(2,1)S(1)} %get-tuple-element.15.pick_ref, f32[64,512]{1,0:T(8,128)S(1)} %collective-permute-done.1.refs_0_, f32[64,512]{1,0:T(8,128)S(1)} %copy-done.1, f32[64,512]{1,0:T(8,128)S(1)} %collective-permute-done.2.refs_2_, ...), custom_call_target="tpu_custom_call" | custom-call | flops 301989888 | bytes 4194304 | tf_op jit(solution)/shard_map/pallas_call | solution.py:83
  16.4 3.9 %collective-permute-done.7.refs_3_ = f32[32,512]{1,0:T(8,128)S(1)} collective-permute-done((f32[32,512]{1,0:T(8,128)S(1)}, f32[32,512]{1,0:T(8,128)S(1)}, u32[]{:S(2)}, u32[]{:S(2)}) %collective-permute-start.7) | collective-permute-done | bytes 65568 | tf_op jit(solution)/shard_map/ppermute | solution.py:127
  20.3 0.0 collective-permute-done.6.refs_2_
  20.3 0.0 collective-permute-done.5.refs_1_
  20.3 0.0 collective-permute-done.4.refs_0_
  20.3 0.5 %shard_map.41 = f32[128,512]{1,0:T(8,128)S(1)} custom-call(bf16[512,1024]{1,0:T(8,128)(2,1)S(1)} %shard_map.38.chosen_ref, bf16[512,224]{1,0:T(8,128)(2,1)S(1)} %get-tuple-element.16.pick_ref, bf16[1536,512]{1,0:T(8,128)(2,1)S(1)} %shard_map.39.right_ref, f32[64,512]{1,0:T(8,128)S(1)} %collective-permute-done.4.refs_0_, ...), custom_call_target="tpu_custom_call" | custom-call | flops 260046848 | bytes 4194304 | tf_op jit(solution)/shard_map/pallas_call | solution.py:111
  20.8 0.1 collective-permute-start.9
  20.9 1.0 %shard_map.40 = (f32[128,512]{1,0:T(8,128)S(1)}, f32[128,512]{1,0:T(8,128)S(1)}, f32[128,512]{1,0:T(8,128)S(1)}) custom-call(bf16[512,1024]{1,0:T(8,128)(2,1)S(1)} %shard_map.38.chosen_ref, bf16[512,224]{1,0:T(8,128)(2,1)S(1)} %get-tuple-element.16.pick_ref, bf16[1536,512]{1,0:T(8,128)(2,1)S(1)} %shard_map.39.right_ref, ...), custom_call_target="tpu_custom_call" | custom-call | flops 780140544 | bytes 4194304 | tf_op jit(solution)/shard_map/pallas_call | solution.py:111
  21.8 0.6 %collective-permute-start.8 = (f32[128,512]{1,0:T(8,128)S(1)}, f32[128,512]{1,0:T(8,128)S(1)}, u32[]{:S(2)}, u32[]{:S(2)}) collective-permute-start(f32[128,512]{1,0:T(8,128)S(1)} %get-tuple-element.19), channel_id=1, source_target_pairs={{0,1},{1,0},{2,3},{3,2},{4,5},{5,4},{6,7},{7,6},{8,9},{9,8},{10,11... | collective-permute-start | bytes 786440 | tf_op jit(solution)/shard_map/ppermute | solution.py:127
  22.4 0.0 collective-permute-done.9
  22.4 1.5 %collective-permute-start.10 = (f32[128,512]{1,0:T(8,128)S(1)}, f32[128,512]{1,0:T(8,128)S(1)}, u32[]{:S(2)}, u32[]{:S(2)}) collective-permute-start(f32[128,512]{1,0:T(8,128)S(1)} %add.47), channel_id=1, source_target_pairs={{0,2},{1,3},{2,0},{3,1},{4,6},{5,7},{6,4},{7,5},{8,10},{9,11},{10,... | collective-permute-start | bytes 786440 | tf_op jit(solution)/shard_map/ppermute | solution.py:127
  23.9 0.0 collective-permute-done.8
  23.9 6.9 %collective-permute-done.10 = f32[128,512]{1,0:T(8,128)S(1)} collective-permute-done((f32[128,512]{1,0:T(8,128)S(1)}, f32[128,512]{1,0:T(8,128)S(1)}, u32[]{:S(2)}, u32[]{:S(2)}) %collective-permute-start.10) | collective-permute-done | bytes 262176 | tf_op jit(solution)/shard_map/ppermute | solution.py:127
  30.8 0.8 %add_add_fusion = f32[128,512]{1,0:T(8,128)} fusion(f32[128,512]{1,0:T(8,128)S(1)} %collective-permute-done.10, f32[128,512]{1,0:T(8,128)S(1)} %get-tuple-element.18, f32[128,512]{1,0:T(8,128)S(1)} %collective-permute-done.8), kind=kLoop, calls=%fused_computation | loop fusion | flops 131072 | bytes 1048576 | tf_op jit(solution)/shard_map/add | solution.py:198
  (5 shorter events, 0.1 us)
Async XLA Ops:
  0.0 15.3 %copy-start = (f32[512,512]{1,0:T(8,128)S(1)}, f32[512,512]{1,0:T(8,128)}, u32[]{:S(2)}) copy-start(f32[512,512]{1,0:T(8,128)} %x_ref.1) | copy-start | bytes 3145732
  0.0 11.3 %collective-permute-start.2 = (f32[64,512]{1,0:T(8,128)}, f32[64,512]{1,0:T(8,128)S(1)}, u32[]{:S(2)}, u32[]{:S(2)}) collective-permute-start(f32[64,512]{1,0:T(8,128)} %refs_1_.1), channel_id=1, source_target_pairs={{0,24},{4,28},{8,16},{12,20},{16,8},{20,12},{24,0},{28,4},{1,25},{... | collective-permute-start | bytes 393224 | tf_op jit(solution)/shard_map/ppermute | solution.py:127
  5.1 7.6 %collective-permute-start.1 = (f32[64,512]{1,0:T(8,128)}, f32[64,512]{1,0:T(8,128)S(1)}, u32[]{:S(2)}, u32[]{:S(2)}) collective-permute-start(f32[64,512]{1,0:T(8,128)} %refs_1_.1), channel_id=1, source_target_pairs={{0,8},{4,12},{8,0},{12,4},{16,24},{20,28},{24,16},{28,20},{1,9},{5... | collective-permute-start | bytes 393224 | tf_op jit(solution)/shard_map/ppermute | solution.py:127
  5.1 5.2 %collective-permute-start.3 = (f32[64,512]{1,0:T(8,128)}, f32[64,512]{1,0:T(8,128)S(1)}, u32[]{:S(2)}, u32[]{:S(2)}) collective-permute-start(f32[64,512]{1,0:T(8,128)} %refs_1_.1), channel_id=1, source_target_pairs={{0,4},{4,0},{8,12},{12,8},{16,20},{20,16},{24,28},{28,24},{1,5},{5... | collective-permute-start | bytes 393224 | tf_op jit(solution)/shard_map/ppermute | solution.py:127
  7.5 7.2 %collective-permute-start = (f32[32,512]{1,0:T(8,128)S(1)}, f32[32,512]{1,0:T(8,128)S(1)}, u32[]{:S(2)}, u32[]{:S(2)}) collective-permute-start(f32[32,512]{1,0:T(8,128)S(1)} %get-tuple-element.66), channel_id=1, source_target_pairs={{0,16},{4,20},{8,24},{12,28},{16,0},{20,4},{24,8},{28,12},{1,17},{... | collective-permute-start | bytes 196616 | tf_op jit(solution)/shard_map/ppermute | solution.py:127
  10.3 10.0 %collective-permute-start.4 = (f32[64,512]{1,0:T(8,128)S(1)}, f32[64,512]{1,0:T(8,128)S(1)}, u32[]{:S(2)}, u32[]{:S(2)}) collective-permute-start(f32[64,512]{1,0:T(8,128)S(1)} %pad_maximum_fusion), channel_id=1, source_target_pairs={{0,16},{4,20},{8,24},{12,28},{16,0},{20,4},{24,8},{28,12},{1,17},{... | collective-permute-start | bytes 393224 | tf_op jit(solution)/shard_map/ppermute | solution.py:127
  11.3 9.0 %collective-permute-start.6 = (f32[64,512]{1,0:T(8,128)S(1)}, f32[64,512]{1,0:T(8,128)S(1)}, u32[]{:S(2)}, u32[]{:S(2)}) collective-permute-start(f32[64,512]{1,0:T(8,128)S(1)} %collective-permute-done.2.refs_2_), channel_id=1, source_target_pairs={{0,4},{4,0},{8,12},{12,8},{16,20},{20,16},{24,28},{28,24},{1,5},{5... | collective-permute-start | bytes 393224 | tf_op jit(solution)/shard_map/ppermute | solution.py:127
  12.6 7.6 %collective-permute-start.5 = (f32[64,512]{1,0:T(8,128)S(1)}, f32[64,512]{1,0:T(8,128)S(1)}, u32[]{:S(2)}, u32[]{:S(2)}) collective-permute-start(f32[64,512]{1,0:T(8,128)S(1)} %collective-permute-done.1.refs_0_), channel_id=1, source_target_pairs={{0,4},{4,0},{8,12},{12,8},{16,20},{20,16},{24,28},{28,24},{1,5},{5... | collective-permute-start | bytes 393224 | tf_op jit(solution)/shard_map/ppermute | solution.py:127
  14.3 1.4 %copy-start.1 = (f32[64,512]{1,0:T(8,128)S(1)}, f32[64,512]{1,0:T(8,128)}, u32[]{:S(2)}) copy-start(f32[64,512]{1,0:T(8,128)} %refs_1_.1) | copy-start | bytes 393220
  14.7 5.6 %collective-permute-start.7 = (f32[32,512]{1,0:T(8,128)S(1)}, f32[32,512]{1,0:T(8,128)S(1)}, u32[]{:S(2)}, u32[]{:S(2)}) collective-permute-start(f32[32,512]{1,0:T(8,128)S(1)} %collective-permute-done.refs_4_), channel_id=1, source_target_pairs={{0,4},{4,0},{8,12},{12,8},{16,20},{20,16},{24,28},{28,24},{1,5},{5... | collective-permute-start | bytes 196616 | tf_op jit(solution)/shard_map/ppermute | solution.py:127
  20.8 1.6 %collective-permute-start.9 = (f32[128,512]{1,0:T(8,128)S(1)}, f32[128,512]{1,0:T(8,128)S(1)}, u32[]{:S(2)}, u32[]{:S(2)}) collective-permute-start(f32[128,512]{1,0:T(8,128)S(1)} %shard_map.41), channel_id=1, source_target_pairs={{0,1},{1,0},{2,3},{3,2},{4,5},{5,4},{6,7},{7,6},{8,9},{9,8},{10,11... | collective-permute-start | bytes 786440 | tf_op jit(solution)/shard_map/ppermute | solution.py:127
  21.8 2.1 %collective-permute-start.8 = (f32[128,512]{1,0:T(8,128)S(1)}, f32[128,512]{1,0:T(8,128)S(1)}, u32[]{:S(2)}, u32[]{:S(2)}) collective-permute-start(f32[128,512]{1,0:T(8,128)S(1)} %get-tuple-element.19), channel_id=1, source_target_pairs={{0,1},{1,0},{2,3},{3,2},{4,5},{5,4},{6,7},{7,6},{8,9},{9,8},{10,11... | collective-permute-start | bytes 786440 | tf_op jit(solution)/shard_map/ppermute | solution.py:127
  22.4 8.4 %collective-permute-start.10 = (f32[128,512]{1,0:T(8,128)S(1)}, f32[128,512]{1,0:T(8,128)S(1)}, u32[]{:S(2)}, u32[]{:S(2)}) collective-permute-start(f32[128,512]{1,0:T(8,128)S(1)} %add.47), channel_id=1, source_target_pairs={{0,2},{1,3},{2,0},{3,1},{4,6},{5,7},{6,4},{7,5},{8,10},{9,11},{10,... | collective-permute-start | bytes 786440 | tf_op jit(solution)/shard_map/ppermute | solution.py:127
